TPU v7x, 32 devices: a whole 2x2x4 slice. The times are simulated.
32 devices in a mesh: dp: 8 (over y, x, core), sub: 4 (over z).
Axes of the slice: x: 2, y: 2, z: 4, core: 2. Of those that a mesh axis runs over, the one named last changes fastest.
Arguments:
- tokens: bfloat16 [25088, 768], P(('dp', 'sub')), may hold values from -6 to 6
- frames_live: int32 [32], P(('dp', 'sub')), may hold values from 1 to 4, as said below
- cotangent: bfloat16 [1024, 768], P(('dp', 'sub')), may hold values from -6 to 6
- ln1_gain: bfloat16 [768], P(('dp', 'sub')), may hold values from 0.5 to 1.5
- ln1_bias: bfloat16 [768], P(('dp', 'sub')), may hold values from -1.25 to 1.25
- w_qkv: bfloat16 [768, 2304], P(('dp', 'sub')), may hold values from -0.21875 to 0.21875
- b_qv: bfloat16 [1536], P(('dp', 'sub')), may hold values from -1.25 to 1.25
- w_out: bfloat16 [768, 768], P(('dp', 'sub')), may hold values from -1.5 to 1.5
- b_out: bfloat16 [768], P(('dp', 'sub')), may hold values from -1.25 to 1.25
- ln2_gain: bfloat16 [768], P(('dp', 'sub')), may hold values from 0.5 to 1.5
- ln2_bias: bfloat16 [768], P(('dp', 'sub')), may hold values from -1.25 to 1.25
- w_in: bfloat16 [768, 3072], P(('dp', 'sub')), may hold values from -0.21875 to 0.21875
- b_in: bfloat16 [3072], P(('dp', 'sub')), may hold values from -1.75 to 1.75
- w_back: bfloat16 [3072, 768], P(('dp', 'sub')), may hold values from -0.21875 to 0.21875
- b_back: bfloat16 [768], P(('dp', 'sub')), may hold values from -1.25 to 1.25
- ln3_gain: bfloat16 [768], P(('dp', 'sub')), may hold values from 0.5 to 1.5
- ln3_bias: bfloat16 [768], P(('dp', 'sub')), may hold values from -1.25 to 1.25
- tl_w1: bfloat16 [768, 64], P(('dp', 'sub')), may hold values from -0.21875 to 0.21875
- tl_b1: bfloat16 [64], replicated, may hold values from -3 to 3
- tl_w2: bfloat16 [64, 8], replicated, may hold values from -1.5 to 1.5
- tl_b2: bfloat16 [8], replicated, may hold values from -3 to 3
Outputs:
- pooled: bfloat16 [1024, 768], P(('dp', 'sub'))
- grad_tokens: float32 [25088, 768], P(('dp', 'sub'))
- grad_ln1_gain: float32 [768], P(('dp', 'sub'))
- grad_ln1_bias: float32 [768], P(('dp', 'sub'))
- grad_w_qkv: float32 [768, 2304], P(('dp', 'sub'))
- grad_b_qv: float32 [1536], P(('dp', 'sub'))
- grad_w_out: float32 [768, 768], P(('dp', 'sub'))
- grad_b_out: float32 [768], P(('dp', 'sub'))
- grad_ln2_gain: float32 [768], P(('dp', 'sub'))
- grad_ln2_bias: float32 [768], P(('dp', 'sub'))
- grad_w_in: float32 [768, 3072], P(('dp', 'sub'))
- grad_b_in: float32 [3072], P(('dp', 'sub'))
- grad_w_back: float32 [3072, 768], P(('dp', 'sub'))
- grad_b_back: float32 [768], P(('dp', 'sub'))
- grad_ln3_gain: float32 [768], P(('dp', 'sub'))
- grad_ln3_bias: float32 [768], P(('dp', 'sub'))
- grad_tl_w1: float32 [768, 64], P(('dp', 'sub'))
- grad_tl_b1: float32 [64], replicated
- grad_tl_w2: float32 [64, 8], replicated
- grad_tl_b2: float32 [8], replicated
- penalty: float32 [], replicated
Inputs may be any that keep to these rules, and one draw needn't show every extreme that they name: `frames_live`: some device holds 4 live frame slots in every draw.
All inputs are finite; a program needn't handle non-finite values.
Results may differ from a plain program's by a relative error of at most 0.006.
Values may be sent and summed in bfloat16 or wider, within the bound.
No kernel may reach another device: no remote copies, remote signals or barrier semaphores. Data moves between devices by JAX's collectives and lax.ppermute only.
A program may use at most 192 MiB of HBM per device.

v0:
```python
import functools
import math

import jax
import jax.numpy as jnp
from jax import lax
from jax.experimental import pallas as pl
from jax.experimental.pallas import tpu as pltpu
from jax.sharding import PartitionSpec as P

HEADS = 12
HDIM = 64
NTOK = 8
P_SIZE = 196
PAD = -(-P_SIZE // 16) * 16
LANES = 128
EPS = 1e-06
AXES = ("dp", "sub")
MIB = 1 << 20
LOW = jnp.bfloat16
WIDE = jnp.float32
exact_mode = lax.Precision.HIGHEST


def dot_nn(left, right, precision=None):
    return lax.dot_general(
        left, right, (((1,), (0,)), ((), ())), precision=precision, preferred_element_type=WIDE
    )


def dot_nt(left, right, precision=None):
    return lax.dot_general(
        left, right, (((1,), (1,)), ((), ())), precision=precision, preferred_element_type=WIDE
    )


def dot_tn(left, right, precision=None):
    return lax.dot_general(
        left, right, (((0,), (0,)), ((), ())), precision=precision, preferred_element_type=WIDE
    )


def gelu_pair(v):
    size = jnp.abs(v)
    t = 1.0 / (1.0 + (0.3275911 * math.sqrt(0.5)) * size)
    bell = jnp.exp(-0.5 * v * v)
    poly = t * (
        0.5 * 0.254829592
        + t
        * (
            0.5 * -0.284496736
            + t * (0.5 * 1.421413741 + t * (0.5 * -1.453152027 + t * (0.5 * 1.061405429)))
        )
    )
    tail = poly * bell
    phi = jnp.where(v >= 0, 1.0 - tail, tail)
    return v * phi, phi + v * bell * (1.0 / math.sqrt(2.0 * math.pi))


def norm_parts(rows):
    center = rows - jnp.mean(rows, axis=-1, keepdims=True)
    scale = lax.rsqrt(jnp.mean(center * center, axis=-1, keepdims=True) + EPS)
    return center * scale, scale


def norm_back(unit, scale, gain, grad):
    inner = grad * gain
    return scale * (
        inner
        - jnp.mean(inner, axis=-1, keepdims=True)
        - unit * jnp.mean(inner * unit, axis=-1, keepdims=True)
    )


def column_sums(rows_in):
    return jnp.sum(rows_in.astype(WIDE), axis=0)


def key_rows_live():
    return lax.broadcasted_iota(jnp.int32, (PAD, PAD), 0) < P_SIZE


def of_head(pair, first):
    low_lanes = lax.broadcasted_iota(jnp.int32, pair.shape, 1) < HDIM
    return jnp.where(low_lanes == first, pair, jnp.zeros_like(pair))


def flip(block):
    return jnp.swapaxes(block.astype(WIDE), 0, 1)


def attend_kernel(width, qkv_ref, out_ref, log_ref):
    live = key_rows_live()
    for pair in range(width // LANES):
        q = qkv_ref[:, pair * LANES : (pair + 1) * LANES]
        k = qkv_ref[:, width + pair * LANES : width + (pair + 1) * LANES]
        v = qkv_ref[:, 2 * width + pair * LANES : 2 * width + (pair + 1) * LANES]
        v_flip = flip(v).astype(LOW)
        halves = []
        for half in range(2):
            scores = jnp.where(live, dot_nt(of_head(k, half == 0), q), -1e30)
            top = jnp.max(scores, axis=0, keepdims=True)
            power = jnp.exp(scores - top)
            total = jnp.sum(power, axis=0, keepdims=True)
            soft = (power * (1.0 / total)).astype(LOW)
            halves.append(dot_nn(v_flip[half * HDIM : (half + 1) * HDIM], soft))
            head = 2 * pair + half
            log_ref[0, head : head + 1, :] = top + jnp.log(total)
        out_ref[:, pair * LANES : (pair + 1) * LANES] = jnp.swapaxes(
            jnp.concatenate(halves, axis=0), 0, 1
        ).astype(LOW)


def attend(qkv, width):
    frames = qkv.shape[0] // PAD
    return pl.pallas_call(
        functools.partial(attend_kernel, width),
        grid=(frames,),
        in_specs=[pl.BlockSpec((PAD, 3 * width), lambda f: (f, 0))],
        out_specs=[
            pl.BlockSpec((PAD, width), lambda f: (f, 0)),
            pl.BlockSpec((1, 16, PAD), lambda f: (f, 0, 0)),
        ],
        out_shape=[
            jax.ShapeDtypeStruct((qkv.shape[0], width), LOW),
            jax.ShapeDtypeStruct((frames, 16, PAD), WIDE),
        ],
        compiler_params=pltpu.CompilerParams(vmem_limit_bytes=24 * MIB),
        cost_estimate=pl.CostEstimate(
            flops=4 * frames * PAD * PAD * width * 4,
            bytes_accessed=qkv.size * 2 + qkv.size,
            transcendentals=frames * PAD * PAD * HEADS,
        ),
        name="attend",
    )(qkv)


def attend_back_kernel(width, qkv_ref, log_ref, grad_ref, out_ref):
    live = key_rows_live()
    for pair in range(width // LANES):
        lanes = slice(pair * LANES, (pair + 1) * LANES)
        q = qkv_ref[:, lanes]
        k = qkv_ref[:, width + pair * LANES : width + (pair + 1) * LANES]
        v = qkv_ref[:, 2 * width + pair * LANES : 2 * width + (pair + 1) * LANES]
        grad = grad_ref[:, lanes]
        k_flip = flip(k).astype(LOW)
        grads_q, grads_k, grads_v = [], [], []
        for half in range(2):
            head = 2 * pair + half
            scores = dot_nt(of_head(k, half == 0), q)
            soft = jnp.where(live, jnp.exp(scores - log_ref[0, head : head + 1, :]), 0.0)
            grads_v.append(dot_nn(soft.astype(LOW), grad))
            grad_soft = dot_nt(of_head(v, half == 0), grad)
            row = jnp.sum(grad_soft * soft, axis=0, keepdims=True)
            grad_scores = (soft * (grad_soft - row)).astype(LOW)
            grads_k.append(dot_nn(grad_scores, q))
            grads_q.append(dot_nn(k_flip[half * HDIM : (half + 1) * HDIM], grad_scores))
        grad_q = jnp.swapaxes(jnp.concatenate(grads_q, axis=0), 0, 1).astype(LOW)
        low_lanes = lax.broadcasted_iota(jnp.int32, (PAD, LANES), 1) < HDIM
        out_ref[:, lanes] = (grad_q.astype(WIDE) * 0.125).astype(LOW)
        out_ref[:, width + pair * LANES : width + (pair + 1) * LANES] = jnp.where(
            low_lanes, grads_k[0], grads_k[1]
        ).astype(LOW)
        out_ref[:, 2 * width + pair * LANES : 2 * width + (pair + 1) * LANES] = jnp.where(
            low_lanes, grads_v[0], grads_v[1]
        ).astype(LOW)


def attend_back(qkv, logs, grad, width):
    frames = qkv.shape[0] // PAD
    return pl.pallas_call(
        functools.partial(attend_back_kernel, width),
        grid=(frames,),
        in_specs=[
            pl.BlockSpec((PAD, 3 * width), lambda f: (f, 0)),
            pl.BlockSpec((1, 16, PAD), lambda f: (f, 0, 0)),
            pl.BlockSpec((PAD, width), lambda f: (f, 0)),
        ],
        out_specs=pl.BlockSpec((PAD, 3 * width), lambda f: (f, 0)),
        out_shape=jax.ShapeDtypeStruct(qkv.shape, LOW),
        compiler_params=pltpu.CompilerParams(vmem_limit_bytes=24 * MIB),
        cost_estimate=pl.CostEstimate(
            flops=10 * frames * PAD * PAD * width * 4,
            bytes_accessed=qkv.size * 5,
            transcendentals=frames * PAD * PAD * HEADS,
        ),
        name="attend_back",
    )(qkv, logs, grad)


def widen_kernel(rows_ref, w_ref, b_ref, low_ref, slope_ref):
    act, slope = gelu_pair(dot_nn(rows_ref[...], w_ref[...]) + b_ref[...])
    low_ref[...] = act.astype(LOW)
    slope_ref[...] = slope.astype(LOW)


def widen(rows, w, b):
    count, width = rows.shape
    hidden = w.shape[1]
    cut = 512
    return pl.pallas_call(
        widen_kernel,
        grid=(hidden // cut,),
        in_specs=[
            pl.BlockSpec((count, width), lambda n: (0, 0)),
            pl.BlockSpec((width, cut), lambda n: (0, n)),
            pl.BlockSpec((1, cut), lambda n: (0, n)),
        ],
        out_specs=[pl.BlockSpec((count, cut), lambda n: (0, n))] * 2,
        out_shape=[jax.ShapeDtypeStruct((count, hidden), LOW)] * 2,
        compiler_params=pltpu.CompilerParams(vmem_limit_bytes=32 * MIB),
        cost_estimate=pl.CostEstimate(
            flops=2 * count * width * hidden,
            bytes_accessed=2 * (rows.size + w.size + 2 * count * hidden),
            transcendentals=2 * count * hidden,
        ),
        name="widen",
    )(rows, w, b)


def learn_kernel(
    live_ref,
    second_ref,
    cot_ref,
    gain_ref,
    bias_ref,
    w_one_ref,
    b_one_ref,
    w_two_ref,
    b_two_ref,
    pooled_ref,
    grad_ref,
    grad_low_ref,
    sums_ref,
    grad_one_ref,
    grad_two_ref,
    small_ref,
):
    frame = pl.program_id(0)
    live = jnp.where(frame < live_ref[0], 1.0, 0.0)
    pair_norm = P_SIZE * NTOK * (NTOK - 1)
    pull = live / (live_ref[1].astype(WIDE) * pair_norm)
    second = second_ref[...]
    gain = gain_ref[...]
    unit, scale = norm_parts(second)
    normed = (unit * gain + bias_ref[...]).astype(LOW)
    w_one = w_one_ref[...]
    act, slope = gelu_pair(dot_nn(normed, w_one) + b_one_ref[...])
    w_two = w_two_ref[...]
    logits = dot_nn(act, w_two, exact_mode) + b_two_ref[...]
    row = lax.broadcasted_iota(jnp.int32, (PAD, LANES), 0)
    lane = lax.broadcasted_iota(jnp.int32, (PAD, LANES), 1)
    inside = (row < P_SIZE) & (lane < NTOK)
    maps = jnp.where(inside, 1.0 / (1.0 + jnp.exp(-logits)), 0.0)
    maps_low = maps.astype(LOW)
    second_low = second.astype(LOW)
    pooled = dot_tn(maps_low, second_low)
    pooled_ref[...] = pooled[:NTOK] * (live / P_SIZE)
    column = jnp.sum(maps, axis=1, keepdims=True)
    crossing = jnp.sum(column * column) - jnp.sum(maps * maps)
    cot = jnp.concatenate([cot_ref[...], jnp.zeros((LANES - NTOK, cot_ref.shape[1]), WIDE)], axis=0)
    cot = cot.astype(LOW)
    grad_maps = dot_nt(second_low, cot) * (live / P_SIZE) + (2.0 * pull) * (column - maps)
    grad_logits = jnp.where(inside, grad_maps * maps * (1.0 - maps), 0.0)
    grad_learn = (dot_nt(grad_logits, w_two, exact_mode) * slope).astype(LOW)
    grad_normed = dot_nt(grad_learn, w_one)
    grad = norm_back(unit, scale, gain, grad_normed) + dot_nn(maps_low, cot) * (live / P_SIZE)
    grad_ref[...] = grad
    grad_low = grad.astype(LOW)
    grad_low_ref[...] = grad_low

    @pl.when(frame == 0)
    def _():
        sums_ref[...] = jnp.zeros_like(sums_ref)
        grad_one_ref[...] = jnp.zeros_like(grad_one_ref)
        grad_two_ref[...] = jnp.zeros_like(grad_two_ref)
        small_ref[...] = jnp.zeros_like(small_ref)

    sums_ref[0:1, :] += jnp.sum(grad_normed * unit, axis=0, keepdims=True)
    sums_ref[1:2, :] += jnp.sum(grad_normed, axis=0, keepdims=True)
    sums_ref[2:3, :] += jnp.sum(grad_low.astype(WIDE), axis=0, keepdims=True)
    grad_one_ref[...] += dot_tn(normed, grad_learn)
    grad_two_ref[...] += dot_tn(act, grad_logits, exact_mode)
    small_ref[0:1, :] += jnp.sum(grad_learn.astype(WIDE), axis=0, keepdims=True)
    small_ref[1:2, :] += jnp.sum(grad_logits, axis=0, keepdims=True)
    small_ref[2:3, :] += jnp.zeros((1, LANES), WIDE) + crossing * pull


def learn(live, second, cot, gain, bias, w_one, b_one, w_two, b_two):
    count, width = second.shape
    frames = count // PAD
    whole = lambda *shape: pl.BlockSpec(shape, lambda f, *_: (0,) * len(shape))
    rows = lambda high, wide: pl.BlockSpec((high, wide), lambda f, *_: (f, 0))
    return pl.pallas_call(
        learn_kernel,
        grid_spec=pltpu.PrefetchScalarGridSpec(
            num_scalar_prefetch=1,
            grid=(frames,),
            in_specs=[
                rows(PAD, width),
                rows(NTOK, width),
                whole(1, width),
                whole(1, width),
                whole(width, LANES),
                whole(1, LANES),
                whole(LANES, LANES),
                whole(1, LANES),
            ],
            out_specs=[
                rows(NTOK, width),
                rows(PAD, width),
                rows(PAD, width),
                whole(8, width),
                whole(width, LANES),
                whole(LANES, LANES),
                whole(8, LANES),
            ],
        ),
        out_shape=[
            jax.ShapeDtypeStruct((frames * NTOK, width), WIDE),
            jax.ShapeDtypeStruct((count, width), WIDE),
            jax.ShapeDtypeStruct((count, width), LOW),
            jax.ShapeDtypeStruct((8, width), WIDE),
            jax.ShapeDtypeStruct((width, LANES), WIDE),
            jax.ShapeDtypeStruct((LANES, LANES), WIDE),
            jax.ShapeDtypeStruct((8, LANES), WIDE),
        ],
        compiler_params=pltpu.CompilerParams(vmem_limit_bytes=24 * MIB),
        cost_estimate=pl.CostEstimate(
            flops=count * width * LANES * 20,
            bytes_accessed=count * width * 10,
            transcendentals=count * LANES * 4,
        ),
        name="learn",
    )(live, second, cot, gain, bias, w_one, b_one, w_two, b_two)


def places():
    dp = lax.axis_index("dp")
    return dp % 2, dp // 2, lax.axis_index("sub")


def swap_cores(array):
    return lax.ppermute(array, AXES, [(i, i ^ 4) for i in range(32)])


def swap_chips(array, first):
    masks = (8, 16) if first else (16, 8)
    return lax.ppermute(array, AXES, [(i, i ^ masks[i // 4 % 2]) for i in range(32)])


def turn(array, step):
    return lax.ppermute(array, AXES, [(i, i // 4 * 4 + (i + step) % 4) for i in range(32)])


def tie(*arrays):
    return lax.optimization_barrier(arrays)


def gather_z(shard):
    z = lax.axis_index("sub")
    parts = [shard] + [turn(shard, step) for step in (1, 2, 3)]
    return parts, z


def join_z(parts, z):
    layers = [lax.select_n((z - place) % 4, *parts) for place in range(4)]
    return jnp.concatenate(layers, axis=0)


def lay_kernel(cuts, at_ref, *refs):
    sources, wholes, sem = refs[:4], refs[4 : 4 + len(cuts)], refs[-1]
    chip, core = at_ref[0], at_ref[1]
    copies = []
    for other in range(2):
        side = core ^ other
        first = 1 + side
        for late in range(2):
            for slot in range(2):
                off = late * (3 - first) + slot * first
                place = (chip ^ off) * 2 + side
                for n, (start, size) in enumerate(cuts):
                    copies.append(
                        pltpu.make_async_copy(
                            sources[2 * other + late].at[slot, :, pl.ds(start, size)],
                            wholes[n].at[place],
                            sem.at[len(copies)],
                        )
                    )
    for copy in copies:
        copy.start()
    for copy in copies:
        copy.wait()


def lay(early, late, early_other, late_other, cuts):
    rows = early.shape[1]
    core, chip, _ = places()
    at = jnp.stack([chip, core]).astype(jnp.int32)
    wholes = pl.pallas_call(
        functools.partial(lay_kernel, cuts),
        grid_spec=pltpu.PrefetchScalarGridSpec(
            num_scalar_prefetch=1,
            grid=(1,),
            in_specs=[pl.BlockSpec(memory_space=pl.ANY)] * 4,
            out_specs=[pl.BlockSpec((8, rows, size), lambda *_: (0, 0, 0)) for _, size in cuts],
            scratch_shapes=[pltpu.SemaphoreType.DMA((8 * len(cuts),))],
        ),
        out_shape=[jax.ShapeDtypeStruct((8, rows, size), LOW) for _, size in cuts],
        compiler_params=pltpu.CompilerParams(vmem_limit_bytes=24 * MIB),
        cost_estimate=pl.CostEstimate(
            flops=0, bytes_accessed=8 * early.size * 2, transcendentals=0
        ),
        name="lay",
    )(at, early, late, early_other, late_other)
    return [whole.reshape(8 * rows, whole.shape[2]) for whole in wholes]


class Sum:
    def __init__(self, fulls):
        self.core, self.chip, self.z = places()
        self.widths = [full.shape[1] for full in fulls]
        self.parts = [f.reshape((4, 2, f.shape[0] // 8) + f.shape[1:]) for f in fulls]
        self.first = 2 - self.core

    def own(self, off):
        at = lax.dynamic_index_in_dim
        parts = [at(at(p, self.chip ^ off, 0, False), self.core, 0, False) for p in self.parts]
        return jnp.concatenate(parts, axis=-1).astype(WIDE)

    def got(self, off):
        return lax.dynamic_index_in_dim(self.from_core, self.chip ^ off, 0, False).astype(WIDE)

    def to_core(self):
        other = [lax.dynamic_index_in_dim(p, 1 - self.core, 1, False) for p in self.parts]
        self.from_core = swap_cores(jnp.concatenate(other, axis=-1))

    def to_chip(self):
        send = [(self.own(off) + self.got(off)).astype(LOW) for off in (self.first, 3)]
        self.from_chip = swap_chips(jnp.stack(send), False)

    def to_last(self):
        second = 3 - self.first
        send = self.own(second) + self.got(second) + self.from_chip[1].astype(WIDE)
        self.from_last = swap_chips(send.astype(LOW), True)

    def to_z(self):
        layer = self.own(0) + self.got(0) + self.from_chip[0].astype(WIDE)
        layer = layer + self.from_last.astype(WIDE)
        layer = layer.reshape((4, layer.shape[0] // 4) + layer.shape[1:])
        at = lambda step: lax.dynamic_index_in_dim(layer, (self.z + step) % 4, 0, False)
        self.layer = at(0)
        self.from_z = [turn(at(step).astype(LOW), step) for step in (1, 2, 3)]

    def total(self):
        whole = self.layer + sum(part.astype(WIDE) for part in self.from_z)
        if len(self.widths) == 1:
            return whole
        ends = [sum(self.widths[: n + 1]) for n in range(len(self.widths))]
        return [whole[:, end - wide : end] for end, wide in zip(ends, self.widths)]


def exchange(rows):
    return lax.all_to_all(rows, AXES, 0, 0, tiled=True)


def share_vectors(quick, vectors):
    if not quick:
        return [lax.all_gather(v, AXES, axis=0, tiled=True) for v in vectors]
    row = jnp.concatenate(vectors).astype(WIDE)
    row = jnp.pad(row, (0, -row.shape[0] % LANES))
    table = exchange(jnp.broadcast_to(row, (32, row.shape[0])))
    whole, at = [], 0
    for v in vectors:
        whole.append(table[:, at : at + v.shape[0]].reshape(-1))
        at += v.shape[0]
    return whole


def sum_vectors(quick, vectors, copied):
    if not quick:
        slices = [lax.psum_scatter(v, AXES, scatter_dimension=0, tiled=True) for v in vectors]
        return slices, lax.psum(copied, AXES)
    flat = jnp.concatenate([array.reshape(-1) for array in copied])
    rows = [v.reshape(32, -1) for v in vectors]
    rows.append(jnp.broadcast_to(flat, (32, flat.shape[0])))
    rows = jnp.concatenate(rows, axis=1)
    row = jnp.sum(exchange(jnp.pad(rows, ((0, 0), (0, -rows.shape[1] % LANES)))), axis=0)
    slices, whole, at = [], [], 0
    for v in vectors:
        size = v.shape[0] // 32
        slices.append(row[at : at + size])
        at += size
    for array in copied:
        whole.append(row[at : at + array.size].reshape(array.shape))
        at += array.size
    return slices, whole


def share_weights(quick, w_qkv, w_mid, cuts, w_back):
    if not quick:
        whole = [lax.all_gather(w, AXES, axis=0, tiled=True) for w in (w_qkv, w_mid, w_back)]
        middle = [whole[1][:, start : start + size] for start, size in cuts]
        return whole[0], middle, whole[2]
    lines = [gather_z(w) for w in (w_qkv, w_mid, w_back)]
    done = []
    for (parts, z), columns in zip(lines, (None, cuts, None)):
        layer = join_z(parts, z)
        early = jnp.stack([layer, swap_chips(layer, True)])
        late = swap_chips(early, False)
        columns = columns or ((0, layer.shape[1]),)
        done.append(lay(early, late, swap_cores(early), swap_cores(late), columns))
    return done[0][0], done[1], done[2][0]


def pad_frames(rows):
    frames = rows.shape[0] // P_SIZE
    rows = rows.reshape(frames, P_SIZE, rows.shape[1])
    return jnp.pad(rows, ((0, 0), (0, PAD - P_SIZE), (0, 0))).reshape(frames * PAD, -1)


def local(
    quick,
    tokens,
    frames_live,
    cotangent,
    ln1_gain,
    ln1_bias,
    w_qkv,
    b_qv,
    w_out,
    b_out,
    ln2_gain,
    ln2_bias,
    w_in,
    b_in,
    w_back,
    b_back,
    ln3_gain,
    ln3_bias,
    tl_w1,
    tl_b1,
    tl_w2,
    tl_b2,
):
    width, hidden = tokens.shape[1], w_in.shape[1]
    frames = tokens.shape[0] // P_SIZE
    learn_wide = tl_w1.shape[1]
    row = lambda v: v.astype(WIDE)[None, :]
    lanes = lambda a: jnp.pad(a, [(0, 0)] * (a.ndim - 1) + [(0, LANES - a.shape[-1])])
    cuts = ((0, width), (width, LANES), (width + LANES, hidden))
    qkv_full, (out_full, learn_full, in_full), back_full = share_weights(
        quick, w_qkv, jnp.concatenate([w_out, lanes(tl_w1), w_in], axis=1), cuts, w_back
    )
    vectors = share_vectors(
        quick,
        (ln1_gain, ln1_bias, b_qv, b_out, ln2_gain, ln2_bias, b_in, b_back, ln3_gain, ln3_bias)
        + (frames_live.astype(LOW),),
    )
    (gain_one, bias_one, qkv_bias, out_bias, gain_two, bias_two, in_bias, back_bias) = (
        v.astype(WIDE) for v in vectors[:8]
    )
    gain_three, bias_three = (v.astype(WIDE) for v in vectors[8:10])
    frame_count = jnp.sum(vectors[10].astype(WIDE))
    live = jnp.stack([frames_live[0], frame_count.astype(jnp.int32)])
    inputs = pad_frames(tokens).astype(WIDE)
    unit_one, scale_one = norm_parts(inputs)
    normed_one = (unit_one * gain_one + bias_one).astype(LOW)
    qkv_shift = jnp.concatenate([qkv_bias[:width], jnp.zeros(width, WIDE), qkv_bias[width:]])
    qkv_scale = jnp.concatenate([jnp.full(width, 0.125, WIDE), jnp.ones(2 * width, WIDE)])
    qkv = ((dot_nn(normed_one, qkv_full) + qkv_shift) * qkv_scale).astype(LOW)
    attended, logs = attend(qkv, width)
    residual_one = inputs + dot_nn(attended, out_full) + out_bias
    unit_two, scale_two = norm_parts(residual_one)
    normed_two = (unit_two * gain_two + bias_two).astype(LOW)
    hidden_low, slope = widen(normed_two, in_full, row(in_bias))
    residual_two = residual_one + dot_nn(hidden_low, back_full) + back_bias
    w_two = jnp.pad(lanes(tl_w2.astype(WIDE)), ((0, LANES - learn_wide), (0, 0)))
    pooled, grad_second, branch_two, sums_three, grad_learn_full, grad_head, small = learn(
        live,
        residual_two,
        cotangent.astype(WIDE),
        row(gain_three),
        row(bias_three),
        learn_full,
        lanes(row(tl_b1)),
        w_two,
        lanes(row(tl_b2)),
    )
    grad_back_full = dot_tn(hidden_low, branch_two).astype(LOW if quick else WIDE)
    if quick:
        sum_back = Sum([grad_back_full])
        sum_back.to_core()
    grad_hidden = (dot_nt(branch_two, back_full) * slope.astype(WIDE)).astype(LOW)
    if quick:
        grad_hidden, sum_back.from_core = tie(grad_hidden, sum_back.from_core)
        sum_back.to_chip()
    grad_in_bias = column_sums(grad_hidden)
    grad_in_full = dot_tn(normed_two, grad_hidden).astype(LOW if quick else WIDE)
    grad_normed_two = dot_nt(grad_hidden, in_full)
    grad_gain_two = jnp.sum(grad_normed_two * unit_two, axis=0)
    grad_bias_two = jnp.sum(grad_normed_two, axis=0)
    grad_first = grad_second + norm_back(unit_two, scale_two, gain_two, grad_normed_two)
    branch_one = grad_first.astype(LOW)
    if quick:
        branch_one, sum_back.from_chip = tie(branch_one, sum_back.from_chip)
        sum_back.to_last()
    grad_out_bias = column_sums(branch_one)
    grad_out_full = dot_tn(attended, branch_one).astype(LOW if quick else WIDE)
    if quick:
        sum_mid = Sum([grad_out_full, grad_learn_full.astype(LOW), grad_in_full])
        sum_mid.to_core()
    grad_attended = dot_nt(branch_one, out_full).astype(LOW)
    if quick:
        grad_attended, sum_back.from_last, sum_mid.from_core = tie(
            grad_attended, sum_back.from_last, sum_mid.from_core
        )
        sum_back.to_z()
        sum_mid.to_chip()
    grad_projected = attend_back(qkv, logs, grad_attended, width)
    if quick:
        grad_projected, sum_mid.from_chip = tie(grad_projected, sum_mid.from_chip)
        sum_mid.to_last()
    grad_qkv_full = dot_tn(normed_one, grad_projected).astype(LOW if quick else WIDE)
    if quick:
        sum_qkv = Sum([grad_qkv_full])
        sum_qkv.to_core()
    grad_qkv_bias = column_sums(grad_projected)
    grad_qkv_bias = jnp.concatenate([grad_qkv_bias[:width], grad_qkv_bias[2 * width :]])
    grad_normed_one = dot_nt(grad_projected, qkv_full)
    if quick:
        grad_normed_one, sum_qkv.from_core = tie(grad_normed_one, sum_qkv.from_core)
        sum_qkv.to_chip()
        sum_mid.to_z()
        sum_qkv.to_last()
        sum_qkv.to_z()
    grad_gain_one = jnp.sum(grad_normed_one * unit_one, axis=0)
    grad_bias_one = jnp.sum(grad_normed_one, axis=0)
    grad_tokens = grad_first + norm_back(unit_one, scale_one, gain_one, grad_normed_one)
    grad_tokens = grad_tokens.reshape(frames, PAD, width)[:, :P_SIZE].reshape(-1, width)
    slices, copied = sum_vectors(
        quick,
        (grad_gain_one, grad_bias_one, grad_qkv_bias, grad_out_bias, grad_gain_two, grad_bias_two)
        + (grad_in_bias, sums_three[2], sums_three[0], sums_three[1]),
        (
            small[0, :learn_wide],
            grad_head[:learn_wide, :NTOK],
            small[1, :NTOK],
            small[2, 0],
        ),
    )
    if quick:
        back_rows, qkv_rows = sum_back.total(), sum_qkv.total()
        out_rows, learn_rows, in_rows = sum_mid.total()
    else:
        scatter = lambda a: lax.psum_scatter(a, AXES, scatter_dimension=0, tiled=True)
        back_rows, qkv_rows = scatter(grad_back_full), scatter(grad_qkv_full)
        out_rows, in_rows = scatter(grad_out_full), scatter(grad_in_full)
        learn_rows = scatter(grad_learn_full)
    return (
        pooled.astype(LOW),
        grad_tokens,
        slices[0],
        slices[1],
        qkv_rows,
        slices[2],
        out_rows,
        slices[3],
        slices[4],
        slices[5],
        in_rows,
        slices[6],
        back_rows,
        slices[7],
        slices[8],
        slices[9],
        learn_rows[:, :learn_wide],
        copied[0],
        copied[1],
        copied[2],
        copied[3],
    )


def solution(mesh):
    quick = dict(mesh.shape) == {"dp": 8, "sub": 4}
    both = P(AXES)
    both_rows = P(AXES, None)
    copied = P()
    return jax.shard_map(
        functools.partial(local, quick),
        mesh=mesh,
        in_specs=(both_rows, both, both_rows, both, both, both_rows, both, both_rows)
        + (both, both, both, both_rows, both, both_rows, both, both, both, both_rows)
        + (copied, copied, copied),
        out_specs=(both_rows, both_rows, both, both, both_rows, both, both_rows)
        + (both, both, both, both_rows, both, both_rows, both, both, both, both_rows)
        + (copied, copied, copied, copied),
        check_vma=False,
    )
```

profile of v0, /device:TPU:0, one launch (start us, length us, event | category | flops | bytes accessed | tf_op | source)
XLA Modules:
  0.0 339.4 jit_solution(7980933380985918136)
XLA Ops:
  0.7 4.1 %collective-permute-start.1 = (bf16[24,2304]{1,0:T(8,128)(2,1)}, bf16[24,2304]{1,0:T(8,128)(2,1)S(1)}, u32[]{:S(2)}, u32[]{:S(2)}) collective-permute-start(bf16[24,2304]{1,0:T(8,128)(2,1)} %param.26), channel_id=1, source_target_pairs={{0,2},{1,3},{2,0},{3,1},{4,6},{5,7},{6,4},{7,5},{8,10},{9,11},{10,... | collective-permute-start | bytes 331784 | tf_op jit(solution)/shard_map/ppermute | solution.py:353
  8.9 2.9 collective-permute-start.9
  12.4 6.8 %concatenate.73 = bf16[337]{0:T(512)(128)(2,1)S(1)} concatenate(bf16[24]{0:T(256)(128)(2,1)} %param.24, bf16[24]{0:T(256)(128)(2,1)} %param.25, bf16[48]{0:T(256)(128)(2,1)} %param.27, bf16[24]{0:T(256)(128)(2,1)} %param.29, bf16[24]{0:T(256)(128)(2,1)} %param.30, bf16[24]{0:T(256)(128)(2,1)} %param.31, bf16[96]{0:T(256)(128)(2,1)} %param.33, bf16[24]{0:T(256)(128)(2,1)} %param.35, ...), dimensions={0} | concatenate | bytes 1348 | tf_op jit(solution)/shard_map/concatenate | solution.py:470
  19.9 3.5 %all-to-all-start = ((f32[32,1,384]{2,1,0:T(1,128)}), f32[32,1,384]{2,1,0:T(1,128)S(1)}, u32[]{:S(2)}, u32[]{:S(2)}) async-start(f32[32,1,384]{2,1,0:T(1,128)} %broadcast_in_dim.12), calls=%async_computation | async-start | bytes 98304 | tf_op jit(solution)/shard_map/all_to_all | solution.py:464
  26.7 2.4 collective-permute-start.15
  37.0 3.8 %collective-permute-done.15 = bf16[96,768]{1,0:T(8,128)(2,1)S(1)} collective-permute-done((bf16[96,768]{1,0:T(8,128)(2,1)S(1)}, bf16[96,768]{1,0:T(8,128)(2,1)S(1)}, u32[]{:S(2)}, u32[]{:S(2)}) %collective-permute-start.15) | collective-permute-done | bytes 147488 | tf_op jit(solution)/shard_map/ppermute | solution.py:353
  40.8 2.5 collective-permute-done.14
  50.2 10.2 %collective-permute-done.17 = bf16[384,768]{1,0:T(8,128)(2,1)} collective-permute-done((bf16[384,768]{1,0:T(8,128)(2,1)}, bf16[384,768]{1,0:T(8,128)(2,1)}, u32[]{:S(2)}, u32[]{:S(2)}) %collective-permute-start.17) | collective-permute-done | bytes 589856 | tf_op jit(solution)/shard_map/ppermute | solution.py:349
  61.7 2.3 collective-permute-start.18
  64.0 2.4 pad.44
  67.5 11.4 %collective-permute-done.11.refs_1_ = bf16[2,96,3968]{2,1,0:T(8,128)(2,1)} collective-permute-done((bf16[2,96,3968]{2,1,0:T(8,128)(2,1)S(1)}, bf16[2,96,3968]{2,1,0:T(8,128)(2,1)}, u32[]{:S(2)}, u32[]{:S(2)}) %collective-permute-start.11) | collective-permute-done | bytes 1523744 | tf_op jit(solution)/shard_map/ppermute | solution.py:349
  83.1 8.4 %collective-permute-done.18.refs_1_ = bf16[2,384,768]{2,1,0:T(8,128)(2,1)} collective-permute-done((bf16[2,384,768]{2,1,0:T(8,128)(2,1)S(1)}, bf16[2,384,768]{2,1,0:T(8,128)(2,1)}, u32[]{:S(2)}, u32[]{:S(2)}) %collective-permute-start.18) | collective-permute-done | bytes 1179680 | tf_op jit(solution)/shard_map/ppermute | solution.py:349
  94.8 2.6 lay.3
  97.4 3.8 %multiply_convert_fusion.1.qkv_ref = bf16[832,2304]{1,0:T(8,128)(2,1)S(1)} fusion(bf16[832,768]{1,0:T(8,128)(2,1)S(1)} %bitcast.218, bf16[768,2304]{1,0:T(8,128)(2,1)S(1)} %bitcast.192, f32[2304]{0:T(1024)S(1)} %copy-done.69, f32[2304]{0:T(1024)S(1)} %pad_maximum_fusion.11), kind=kOutput, calls=%fused_computation.3 | convolution fusion | flops 2950152192 | bytes 8669184 | tf_op jit(solution)/shard_map/dot_general | solution.py:26
  101.2 11.0 %attend.1 = (bf16[832,768]{1,0:T(8,128)(2,1)S(1)}, f32[4,16,208]{2,1,0:T(8,128)S(1)}) custom-call(bf16[832,2304]{1,0:T(8,128)(2,1)S(1)} %multiply_convert_fusion.1.qkv_ref), custom_call_target="tpu_custom_call" | custom-call | flops 2126512128 | bytes 5750784 | tf_op jit(solution)/shard_map/attend/pallas_call | solution.py:116
  112.3 2.1 lay.5
  114.5 4.6 %lay.4 = (bf16[8,96,768]{2,1,0:T(8,128)(2,1)S(1)}, bf16[8,96,128]{2,1,0:T(8,128)(2,1)S(1)}, bf16[8,96,3072]{2,1,0:T(8,128)(2,1)S(1)}) custom-call(s32[2]{0:T(128)S(1)} %pad_add_fusion.1.at_ref, bf16[2,96,3968]{2,1,0:T(8,128)(2,1)S(1)} %pad_maximum_fusion.1.refs_0_, bf16[2,96,3968]{2,1,0:T(8,128)(2,1)} %collective-permute-done.11.refs_1_, ...), custom_call_target="tpu_custom_call" | custom-call | bytes 12189696 | tf_op jit(solution)/shard_map/lay/pallas_call | solution.py:400
  121.7 13.7 %widen.1 = (bf16[832,3072]{1,0:T(8,128)(2,1)S(1)}, bf16[832,3072]{1,0:T(8,128)(2,1)S(1)}) custom-call(bf16[832,768]{1,0:T(8,128)(2,1)S(1)} %add_convert_fusion.1.rows_ref, bf16[768,3072]{1,0:T(8,128)(2,1)S(1)} %bitcast.194, f32[1,3072]{1,0:T(1,128)S(1)} %broadcast_in_dim_reshape.6.b_ref), custom_call_target="tpu_custom_call" | custom-call | flops 3925868544 | bytes 16220160 | tf_op jit(solution)/shard_map/widen/pallas_call | solution.py:201
  135.5 4.1 %add_add_fusion.second_ref = f32[832,768]{1,0:T(8,128)S(1)} fusion(f32[832,768]{1,0:T(8,128)S(1)} %bitcast_add_fusion, bf16[832,3072]{1,0:T(8,128)(2,1)S(1)} %get-tuple-element.49, bf16[3072,768]{1,0:T(8,128)(2,1)S(1)} %bitcast.190, f32[768]{0:T(1024)S(1)} %add.472, f32[768]{0:T(1024)S(1)} %add.464), kind=kOutput, calls=%fused_computation.27 | convolution fusion | flops 3927785472 | bytes 14948352 | tf_op jit(solution)/shard_map/dot_general | solution.py:26
  139.7 10.5 %learn.1 = (f32[32,768]{1,0:T(8,128)S(1)}, f32[832,768]{1,0:T(8,128)S(1)}, bf16[832,768]{1,0:T(8,128)(2,1)S(1)}, f32[8,768]{1,0:T(8,128)S(1)}, f32[768,128]{1,0:...) custom-call(s32[2]{0:T(128)S(1)} %pad_add_fusion.live_ref, f32[832,768]{1,0:T(8,128)S(1)} %add_add_fusion.second_ref, ...), custom_call_target="tpu_custom_call" | custom-call | flops 1635778560 | bytes 6389760 | tf_op jit(solution)/shard_map/learn/pallas_call | solution.py:294
  150.2 5.5 %convolution_convert_fusion.2 = bf16[3072,768]{1,0:T(8,128)(2,1)S(1)} fusion(bf16[832,3072]{1,0:T(8,128)(2,1)S(1)} %get-tuple-element.49, bf16[832,768]{1,0:T(8,128)(2,1)S(1)} %get-tuple-element.53), kind=kOutput, calls=%fused_computation.6 | convolution fusion | flops 3928227840 | bytes 11108352 | tf_op jit(solution)/shard_map/dot_general | solution.py:38
  155.7 2.1 copy-done.24
  159.5 8.5 %multiply_convert_fusion = bf16[832,3072]{1,0:T(8,128)(2,1)S(1)} fusion(bf16[832,3072]{1,0:T(8,128)(2,1)} %copy-done.13, bf16[832,768]{1,0:T(8,128)(2,1)} %copy-done.12, bf16[3072,768]{1,0:T(8,128)(2,1)} %bitcast.191), kind=kOutput, calls=%fused_computation.1 | convolution fusion | flops 3933536256 | bytes 16220160 | tf_op jit(solution)/shard_map/dot_general | solution.py:32
  168.1 9.6 %multiply_reduce_fusion = (f32[768]{0:T(1024)}, f32[832]{0:T(1024)S(1)}, f32[832]{0:T(1024)S(1)}, f32[768]{0:T(1024)}, f32[832,768]{1,0:T(8,128)S(1)}) fusion(f32[832]{0:T(1024)S(1)} %add_rsqrt_fusion, f32[832]{0:T(1024)S(1)} %broadcast_multiply_fusion.4, f32[832,768]{1,0:T(8,128)S(1)} %copy-done.18, f32[768]{0:T(1024)S(1)} %add.464, f32[768]{0:T(1024)S(1)} %mul.127, ...), kind=kOutput, calls=%fused_computation.19 | convolution fusion | flops 3932255232 | bytes 14967808 | tf_op jit(solution)/shard_map/dot_general | solution.py:32
  177.7 5.6 %convolution_convert_fusion.1 = bf16[768,3072]{1,0:T(8,128)(2,1)S(1)} fusion(bf16[832,768]{1,0:T(8,128)(2,1)S(1)} %copy-done.4, bf16[832,3072]{1,0:T(8,128)(2,1)S(1)} %multiply_convert_fusion), kind=kOutput, calls=%fused_computation.5 | convolution fusion | flops 3928227840 | bytes 11108352 | tf_op jit(solution)/shard_map/dot_general | solution.py:38
  183.3 3.6 %fusion.14 = (bf16[1,384,768]{2,1,0:T(8,128)(2,1)S(1)}, bf16[1,384,768]{2,1,0:T(8,128)(2,1)S(1)}) fusion(bf16[4,384,768]{2,1,0:T(8,128)(2,1)} %collective-permute-done.21, s32[]{:T(128)S(6)} %select_n.575, bf16[4,2,384,768]{3,2,1,0:T(8,128)(2,1)} %bitcast.203, s32[]{:T(128)S(6)} %select_n.576, s32[]{:T(128)S(6)} %select_n.578, s32[]{:T(128)S(6)} %select_n.579, ...), kind=kLoop, calls=%fused_computation.62 | loop fusion | flops 2359296 | bytes 3538964 | tf_op jit(solution)/shard_map/convert_element_type | solution.py:439
  188.4 2.3 fusion.36
  190.6 12.6 %collective-permute-done.22 = bf16[2,384,768]{2,1,0:T(8,128)(2,1)S(1)} collective-permute-done((bf16[2,384,768]{2,1,0:T(8,128)(2,1)S(1)}, bf16[2,384,768]{2,1,0:T(8,128)(2,1)S(1)}, u32[]{:S(2)}, u32[]{:S(2)}) %collective-permute-start.22) | collective-permute-done | bytes 1179680 | tf_op jit(solution)/shard_map/ppermute | solution.py:349
  213.4 2.4 fusion.12
  217.6 3.1 dynamic-slice_bitcast_fusion.4
  222.9 3.3 convolution_convert_fusion.3.grad_ref
  236.0 3.2 collective-permute-start.38
  239.2 3.0 collective-permute-start.37
  242.1 1.9 collective-permute-start.36
  244.1 16.2 %attend_back.1 = bf16[832,2304]{1,0:T(8,128)(2,1)S(1)} custom-call(bf16[832,2304]{1,0:T(8,128)(2,1)S(1)} %copy-done.11, f32[4,16,208]{2,1,0:T(8,128)S(1)} %get-tuple-element.56.log_ref, bf16[832,768]{1,0:T(8,128)(2,1)S(1)} %convolution_convert_fusion.3.grad_ref), custom_call_target="tpu_custom_call" | custom-call | flops 5316280320 | bytes 9584640 | tf_op jit(solution)/shard_map/attend_back/pallas_call | solution.py:171
  261.1 4.7 %fusion.41 = f32[832,768]{1,0:T(8,128)} fusion(bf16[832,2304]{1,0:T(8,128)(2,1)S(1)} %attend_back.1, bf16[768,2304]{1,0:T(8,128)(2,1)S(1)} %bitcast.193), kind=kOutput, calls=%fused_computation.166 | convolution fusion | flops 2944401408 | bytes 9928704 | tf_op jit(solution)/shard_map/dot_general | solution.py:32
  265.9 4.2 %convolution_convert_fusion = bf16[768,2304]{1,0:T(8,128)(2,1)S(1)} fusion(bf16[832,2304]{1,0:T(8,128)(2,1)S(1)} %attend_back.1, f32[832,768]{1,0:T(8,128)S(1)} %copy-done.20, f32[768]{0:T(1024)S(1)} %copy-done.62, f32[768]{0:T(1024)S(1)} %copy-done.51), kind=kOutput, calls=%fused_computation.4 | convolution fusion | flops 2948087808 | bytes 9934848 | tf_op jit(solution)/shard_map/dot_general | solution.py:38
  270.1 3.7 %fusion.7 = bf16[96,3968]{1,0:T(8,128)(2,1)} fusion(bf16[96,3072]{1,0:T(8,128)(2,1)S(1)} %copy-done.29, bf16[96,128]{1,0:T(8,128)(2,1)S(1)} %copy-done.40, bf16[96,768]{1,0:T(8,128)(2,1)S(1)} %copy-done.36, bf16[2,96,3968]{2,1,0:T(8,128)(2,1)} %collective-permute-done.25, bf16[4,96,3968]{2,1,0:T(8,128)(2,1)} %collective-permute-done.24, s32[]{:T(128)S(6)} %select_n.581), kind=kLoop, calls=%fused_computation.42 | loop fusion | flops 4190208 | bytes 3047428 | tf_op jit(solution)/shard_map/convert_element_type | solution.py:445
  281.8 4.0 %collective-permute-done.32 = bf16[96,3968]{1,0:T(8,128)(2,1)} collective-permute-done((bf16[96,3968]{1,0:T(8,128)(2,1)}, bf16[96,3968]{1,0:T(8,128)(2,1)}, u32[]{:S(2)}, u32[]{:S(2)}) %collective-permute-start.32) | collective-permute-done | bytes 761888 | tf_op jit(solution)/shard_map/ppermute | solution.py:349
  285.8 2.2 fusion.8
  288.1 1.9 collective-permute-start.35
  292.9 2.4 collective-permute-done.35
  295.3 10.2 %collective-permute-done.34 = bf16[24,3968]{1,0:T(8,128)(2,1)S(1)} collective-permute-done((bf16[24,3968]{1,0:T(8,128)(2,1)S(1)}, bf16[24,3968]{1,0:T(8,128)(2,1)S(1)}, u32[]{:S(2)}, u32[]{:S(2)}) %collective-permute-start.34) | collective-permute-done | bytes 190496 | tf_op jit(solution)/shard_map/ppermute | solution.py:353
  308.7 2.1 fusion.15
  312.7 3.7 %all-to-all-start.1 = ((f32[32,1,1024]{2,1,0:T(1,128)}), f32[32,1,1024]{2,1,0:T(1,128)S(1)}, u32[]{:S(2)}, u32[]{:S(2)}) async-start(f32[32,1,1024]{2,1,0:T(1,128)} %all_to_all.14), calls=%async_computation.1 | async-start | bytes 262144 | tf_op jit(solution)/shard_map/all_to_all | solution.py:464
  316.3 3.0 multiply_add_fusion
  321.1 3.6 %all-to-all-done.1 = f32[32,1,1024]{2,1,0:T(1,128)S(1)} async-done(((f32[32,1,1024]{2,1,0:T(1,128)}), f32[32,1,1024]{2,1,0:T(1,128)S(1)}, u32[]{:S(2)}, u32[]{:S(2)}) %all-to-all-start.1) | async-done | bytes 131104 | tf_op jit(solution)/shard_map/all_to_all | solution.py:464
  333.2 5.1 %collective-permute-done.30 = bf16[24,2304]{1,0:T(8,128)(2,1)S(1)} collective-permute-done((bf16[24,2304]{1,0:T(8,128)(2,1)S(1)}, bf16[24,2304]{1,0:T(8,128)(2,1)S(1)}, u32[]{:S(2)}, u32[]{:S(2)}) %collective-permute-start.30) | collective-permute-done | bytes 110624 | tf_op jit(solution)/shard_map/ppermute | solution.py:353
  (328 shorter events, 88.9 us)
Async XLA Ops:
  0.7 29.9 %copy-start.39 = (bf16[24,2304]{1,0:T(8,128)(2,1)S(1)}, bf16[24,2304]{1,0:T(8,128)(2,1)}, u32[]{:S(2)}) copy-start(bf16[24,2304]{1,0:T(8,128)(2,1)} %param.26) | copy-start | bytes 331780
  0.7 26.0 %copy-start.38 = (bf16[96,768]{1,0:T(8,128)(2,1)S(1)}, bf16[96,768]{1,0:T(8,128)(2,1)}, u32[]{:S(2)}) copy-start(bf16[96,768]{1,0:T(8,128)(2,1)} %param.34) | copy-start | bytes 442372
  0.7 24.2 %collective-permute-start.1 = (bf16[24,2304]{1,0:T(8,128)(2,1)}, bf16[24,2304]{1,0:T(8,128)(2,1)S(1)}, u32[]{:S(2)}, u32[]{:S(2)}) collective-permute-start(bf16[24,2304]{1,0:T(8,128)(2,1)} %param.26), channel_id=1, source_target_pairs={{0,2},{1,3},{2,0},{3,1},{4,6},{5,7},{6,4},{7,5},{8,10},{9,11},{10,... | collective-permute-start | bytes 331784 | tf_op jit(solution)/shard_map/ppermute | solution.py:353
  4.8 21.9 %collective-permute-start.2 = (bf16[24,2304]{1,0:T(8,128)(2,1)}, bf16[24,2304]{1,0:T(8,128)(2,1)S(1)}, u32[]{:S(2)}, u32[]{:S(2)}) collective-permute-start(bf16[24,2304]{1,0:T(8,128)(2,1)} %param.26), channel_id=1, source_target_pairs={{0,3},{1,0},{2,1},{3,2},{4,7},{5,4},{6,5},{7,6},{8,11},{9,8},{10,9... | collective-permute-start | bytes 331784 | tf_op jit(solution)/shard_map/ppermute | solution.py:353
  6.1 23.0 %collective-permute-start = (bf16[24,2304]{1,0:T(8,128)(2,1)}, bf16[24,2304]{1,0:T(8,128)(2,1)S(1)}, u32[]{:S(2)}, u32[]{:S(2)}) collective-permute-start(bf16[24,2304]{1,0:T(8,128)(2,1)} %param.26), channel_id=1, source_target_pairs={{0,1},{1,2},{2,3},{3,0},{4,5},{5,6},{6,7},{7,4},{8,9},{9,10},{10,1... | collective-permute-start | bytes 331784 | tf_op jit(solution)/shard_map/ppermute | solution.py:353
  7.7 26.7 %copy-start.30 = (bf16[24,3072]{1,0:T(8,128)(2,1)S(1)}, bf16[24,3072]{1,0:T(8,128)(2,1)}, u32[]{:S(2)}) copy-start(bf16[24,3072]{1,0:T(8,128)(2,1)} %param.32) | copy-start | bytes 442372
  7.8 26.7 %copy-start.37 = (bf16[24,768]{1,0:T(8,128)(2,1)S(1)}, bf16[24,768]{1,0:T(8,128)(2,1)}, u32[]{:S(2)}) copy-start(bf16[24,768]{1,0:T(8,128)(2,1)} %param.28) | copy-start | bytes 110596
  7.8 26.7 %copy-start.57 = (bf16[24,64]{1,0:T(8,128)(2,1)S(1)}, bf16[24,64]{1,0:T(8,128)(2,1)}, u32[]{:S(2)}) copy-start(bf16[24,64]{1,0:T(8,128)(2,1)} %param.38) | copy-start | bytes 9220
  7.8 22.9 %collective-permute-start.8 = (bf16[24,3968]{1,0:T(8,128)(2,1)S(1)}, bf16[24,3968]{1,0:T(8,128)(2,1)S(1)}, u32[]{:S(2)}, u32[]{:S(2)}) collective-permute-start(bf16[24,3968]{1,0:T(8,128)(2,1)S(1)} %fusion.22), channel_id=1, source_target_pairs={{0,2},{1,3},{2,0},{3,1},{4,6},{5,7},{6,4},{7,5},{8,10},{9,11},{10,... | collective-permute-start | bytes 571400 | tf_op jit(solution)/shard_map/ppermute | solution.py:353
  8.9 22.5 %collective-permute-start.9 = (bf16[24,3968]{1,0:T(8,128)(2,1)S(1)}, bf16[24,3968]{1,0:T(8,128)(2,1)S(1)}, u32[]{:S(2)}, u32[]{:S(2)}) collective-permute-start(bf16[24,3968]{1,0:T(8,128)(2,1)S(1)} %fusion.22), channel_id=1, source_target_pairs={{0,3},{1,0},{2,1},{3,2},{4,7},{5,4},{6,5},{7,6},{8,11},{9,8},{10,9... | collective-permute-start | bytes 571400 | tf_op jit(solution)/shard_map/ppermute | solution.py:353
  19.9 46.8 %all-to-all-start = ((f32[32,1,384]{2,1,0:T(1,128)}), f32[32,1,384]{2,1,0:T(1,128)S(1)}, u32[]{:S(2)}, u32[]{:S(2)}) async-start(f32[32,1,384]{2,1,0:T(1,128)} %broadcast_in_dim.12), calls=%async_computation | async-start | bytes 98304 | tf_op jit(solution)/shard_map/all_to_all | solution.py:464
  24.9 24.8 %copy-start.14 = (bf16[4,196,768]{2,1,0:T(8,128)(2,1)}, bf16[4,196,768]{2,1,0:T(8,128)(2,1)S(1)}, u32[]{:S(2)}) copy-start(bf16[4,196,768]{2,1,0:T(8,128)(2,1)S(1)} %reshape.460) | copy-start | bytes 3612676
  24.9 9.6 %collective-permute-start.7 = (bf16[24,3968]{1,0:T(8,128)(2,1)S(1)}, bf16[24,3968]{1,0:T(8,128)(2,1)S(1)}, u32[]{:S(2)}, u32[]{:S(2)}) collective-permute-start(bf16[24,3968]{1,0:T(8,128)(2,1)S(1)} %fusion.22), channel_id=1, source_target_pairs={{0,1},{1,2},{2,3},{3,0},{4,5},{5,6},{6,7},{7,4},{8,9},{9,10},{10,1... | collective-permute-start | bytes 571400 | tf_op jit(solution)/shard_map/ppermute | solution.py:353
  26.7 14.1 %collective-permute-start.15 = (bf16[96,768]{1,0:T(8,128)(2,1)S(1)}, bf16[96,768]{1,0:T(8,128)(2,1)S(1)}, u32[]{:S(2)}, u32[]{:S(2)}) collective-permute-start(bf16[96,768]{1,0:T(8,128)(2,1)S(1)} %copy-done.38), channel_id=1, source_target_pairs={{0,2},{1,3},{2,0},{3,1},{4,6},{5,7},{6,4},{7,5},{8,10},{9,11},{10,... | collective-permute-start | bytes 442376 | tf_op jit(solution)/shard_map/ppermute | solution.py:353
  29.1 11.7 %collective-permute-start.16 = (bf16[96,768]{1,0:T(8,128)(2,1)S(1)}, bf16[96,768]{1,0:T(8,128)(2,1)S(1)}, u32[]{:S(2)}, u32[]{:S(2)}) collective-permute-start(bf16[96,768]{1,0:T(8,128)(2,1)S(1)} %copy-done.38), channel_id=1, source_target_pairs={{0,3},{1,0},{2,1},{3,2},{4,7},{5,4},{6,5},{7,6},{8,11},{9,8},{10,9... | collective-permute-start | bytes 442376 | tf_op jit(solution)/shard_map/ppermute | solution.py:353
  30.7 12.6 %collective-permute-start.14 = (bf16[96,768]{1,0:T(8,128)(2,1)S(1)}, bf16[96,768]{1,0:T(8,128)(2,1)S(1)}, u32[]{:S(2)}, u32[]{:S(2)}) collective-permute-start(bf16[96,768]{1,0:T(8,128)(2,1)S(1)} %copy-done.38), channel_id=1, source_target_pairs={{0,1},{1,2},{2,3},{3,0},{4,5},{5,6},{6,7},{7,4},{8,9},{9,10},{10,1... | collective-permute-start | bytes 442376 | tf_op jit(solution)/shard_map/ppermute | solution.py:353
  31.3 14.8 %collective-permute-start.3 = (bf16[96,2304]{1,0:T(8,128)(2,1)S(1)}, bf16[96,2304]{1,0:T(8,128)(2,1)S(1)}, u32[]{:S(2)}, u32[]{:S(2)}) collective-permute-start(bf16[96,2304]{1,0:T(8,128)(2,1)S(1)} %get-tuple-element.164), channel_id=1, source_target_pairs={{0,8},{1,9},{2,10},{3,11},{4,20},{5,21},{6,22},{7,23},{8,0},{9,1},... | collective-permute-start | bytes 1327112 | tf_op jit(solution)/shard_map/ppermute | solution.py:349
  34.9 13.7 %collective-permute-start.10 = (bf16[96,3968]{1,0:T(8,128)(2,1)S(1)}, bf16[96,3968]{1,0:T(8,128)(2,1)S(1)}, u32[]{:S(2)}, u32[]{:S(2)}) collective-permute-start(bf16[96,3968]{1,0:T(8,128)(2,1)S(1)} %get-tuple-element.152), channel_id=1, source_target_pairs={{0,8},{1,9},{2,10},{3,11},{4,20},{5,21},{6,22},{7,23},{8,0},{9,1},... | collective-permute-start | bytes 2285576 | tf_op jit(solution)/shard_map/ppermute | solution.py:349
  44.5 15.9 %collective-permute-start.17 = (bf16[384,768]{1,0:T(8,128)(2,1)}, bf16[384,768]{1,0:T(8,128)(2,1)}, u32[]{:S(2)}, u32[]{:S(2)}) collective-permute-start(bf16[384,768]{1,0:T(8,128)(2,1)} %get-tuple-element.158), channel_id=1, source_target_pairs={{0,8},{1,9},{2,10},{3,11},{4,20},{5,21},{6,22},{7,23},{8,0},{9,1},... | collective-permute-start | bytes 1769480 | tf_op jit(solution)/shard_map/ppermute | solution.py:349
  47.1 19.5 %collective-permute-start.4 = (bf16[2,96,2304]{2,1,0:T(8,128)(2,1)}, bf16[2,96,2304]{2,1,0:T(8,128)(2,1)}, u32[]{:S(2)}, u32[]{:S(2)}) collective-permute-start(bf16[2,96,2304]{2,1,0:T(8,128)(2,1)} %pad_maximum_fusion.5.refs_0_), channel_id=1, source_target_pairs={{0,16},{1,17},{2,18},{3,19},{4,12},{5,13},{6,14},{7,15},{8,24},{9,... | collective-permute-start | bytes 2654216 | tf_op jit(solution)/shard_map/ppermute | solution.py:349
  48.8 30.1 %collective-permute-start.11 = (bf16[2,96,3968]{2,1,0:T(8,128)(2,1)S(1)}, bf16[2,96,3968]{2,1,0:T(8,128)(2,1)}, u32[]{:S(2)}, u32[]{:S(2)}) collective-permute-start(bf16[2,96,3968]{2,1,0:T(8,128)(2,1)S(1)} %pad_maximum_fusion.1.refs_0_), channel_id=1, source_target_pairs={{0,16},{1,17},{2,18},{3,19},{4,12},{5,13},{6,14},{7,15},{8,24},{9,... | collective-permute-start | bytes 4571144 | tf_op jit(solution)/shard_map/ppermute | solution.py:349
  61.7 29.8 %collective-permute-start.18 = (bf16[2,384,768]{2,1,0:T(8,128)(2,1)S(1)}, bf16[2,384,768]{2,1,0:T(8,128)(2,1)}, u32[]{:S(2)}, u32[]{:S(2)}) collective-permute-start(bf16[2,384,768]{2,1,0:T(8,128)(2,1)S(1)} %pad_maximum_fusion.3.refs_0_), channel_id=1, source_target_pairs={{0,16},{1,17},{2,18},{3,19},{4,12},{5,13},{6,14},{7,15},{8,24},{9,... | collective-permute-start | bytes 3538952 | tf_op jit(solution)/shard_map/ppermute | solution.py:349
  66.5 30.8 %copy-start.59 = (f32[4,208]{1,0:T(4,128)}, f32[4,208]{1,0:T(4,128)S(1)}, u32[]{:S(2)}) copy-start(f32[4,208]{1,0:T(4,128)S(1)} %add_rsqrt_fusion.1) | copy-start | bytes 9988
  66.5 16.5 %collective-permute-start.5 = (bf16[2,96,2304]{2,1,0:T(8,128)(2,1)}, bf16[2,96,2304]{2,1,0:T(8,128)(2,1)}, u32[]{:S(2)}, u32[]{:S(2)}) collective-permute-start(bf16[2,96,2304]{2,1,0:T(8,128)(2,1)} %pad_maximum_fusion.5.refs_0_), channel_id=1, source_target_pairs={{0,4},{1,5},{2,6},{3,7},{4,0},{5,1},{6,2},{7,3},{8,12},{9,13},{10,... | collective-permute-start | bytes 2654216 | tf_op jit(solution)/shard_map/ppermute | solution.py:344
  66.7 28.1 %collective-permute-start.6 = (bf16[2,96,2304]{2,1,0:T(8,128)(2,1)}, bf16[2,96,2304]{2,1,0:T(8,128)(2,1)}, u32[]{:S(2)}, u32[]{:S(2)}) collective-permute-start(bf16[2,96,2304]{2,1,0:T(8,128)(2,1)} %collective-permute-done.4.refs_1_), channel_id=1, source_target_pairs={{0,4},{1,5},{2,6},{3,7},{4,0},{5,1},{6,2},{7,3},{8,12},{9,13},{10,... | collective-permute-start | bytes 2654216 | tf_op jit(solution)/shard_map/ppermute | solution.py:344
  67.4 47.1 %collective-permute-start.12 = (bf16[2,96,3968]{2,1,0:T(8,128)(2,1)S(1)}, bf16[2,96,3968]{2,1,0:T(8,128)(2,1)}, u32[]{:S(2)}, u32[]{:S(2)}) collective-permute-start(bf16[2,96,3968]{2,1,0:T(8,128)(2,1)S(1)} %pad_maximum_fusion.1.refs_0_), channel_id=1, source_target_pairs={{0,4},{1,5},{2,6},{3,7},{4,0},{5,1},{6,2},{7,3},{8,12},{9,13},{10,... | collective-permute-start | bytes 4571144 | tf_op jit(solution)/shard_map/ppermute | solution.py:344
  78.9 35.6 %collective-permute-start.13 = (bf16[2,96,3968]{2,1,0:T(8,128)(2,1)}, bf16[2,96,3968]{2,1,0:T(8,128)(2,1)}, u32[]{:S(2)}, u32[]{:S(2)}) collective-permute-start(bf16[2,96,3968]{2,1,0:T(8,128)(2,1)} %collective-permute-done.11.refs_1_), channel_id=1, source_target_pairs={{0,4},{1,5},{2,6},{3,7},{4,0},{5,1},{6,2},{7,3},{8,12},{9,13},{10,... | collective-permute-start | bytes 4571144 | tf_op jit(solution)/shard_map/ppermute | solution.py:344
  83.1 29.3 %collective-permute-start.19 = (bf16[2,384,768]{2,1,0:T(8,128)(2,1)S(1)}, bf16[2,384,768]{2,1,0:T(8,128)(2,1)S(1)}, u32[]{:S(2)}, u32[]{:S(2)}) collective-permute-start(bf16[2,384,768]{2,1,0:T(8,128)(2,1)S(1)} %pad_maximum_fusion.3.refs_0_), channel_id=1, source_target_pairs={{0,4},{1,5},{2,6},{3,7},{4,0},{5,1},{6,2},{7,3},{8,12},{9,13},{10,... | collective-permute-start | bytes 3538952 | tf_op jit(solution)/shard_map/ppermute | solution.py:344
  91.5 20.8 %collective-permute-start.20 = (bf16[2,384,768]{2,1,0:T(8,128)(2,1)}, bf16[2,384,768]{2,1,0:T(8,128)(2,1)S(1)}, u32[]{:S(2)}, u32[]{:S(2)}) collective-permute-start(bf16[2,384,768]{2,1,0:T(8,128)(2,1)} %collective-permute-done.18.refs_1_), channel_id=1, source_target_pairs={{0,4},{1,5},{2,6},{3,7},{4,0},{5,1},{6,2},{7,3},{8,12},{9,13},{10,... | collective-permute-start | bytes 3538952 | tf_op jit(solution)/shard_map/ppermute | solution.py:344
  159.4 8.7 %collective-permute-start.21 = (bf16[4,384,768]{2,1,0:T(8,128)(2,1)}, bf16[4,384,768]{2,1,0:T(8,128)(2,1)}, u32[]{:S(2)}, u32[]{:S(2)}) collective-permute-start(bf16[4,384,768]{2,1,0:T(8,128)(2,1)} %dynamic-slice_bitcast_fusion.1), channel_id=1, source_target_pairs={{0,4},{1,5},{2,6},{3,7},{4,0},{5,1},{6,2},{7,3},{8,12},{9,13},{10,... | collective-permute-start | bytes 7077896 | tf_op jit(solution)/shard_map/ppermute | solution.py:344
  187.0 16.3 %collective-permute-start.22 = (bf16[2,384,768]{2,1,0:T(8,128)(2,1)S(1)}, bf16[2,384,768]{2,1,0:T(8,128)(2,1)S(1)}, u32[]{:S(2)}, u32[]{:S(2)}) collective-permute-start(bf16[2,384,768]{2,1,0:T(8,128)(2,1)S(1)} %pad_maximum_fusion.4), channel_id=1, source_target_pairs={{0,16},{1,17},{2,18},{3,19},{4,12},{5,13},{6,14},{7,15},{8,24},{9,... | collective-permute-start | bytes 3538952 | tf_op jit(solution)/shard_map/ppermute | solution.py:349
  206.7 19.5 %collective-permute-start.24 = (bf16[4,96,3968]{2,1,0:T(8,128)(2,1)}, bf16[4,96,3968]{2,1,0:T(8,128)(2,1)}, u32[]{:S(2)}, u32[]{:S(2)}) collective-permute-start(bf16[4,96,3968]{2,1,0:T(8,128)(2,1)} %pad_maximum_fusion), channel_id=1, source_target_pairs={{0,4},{1,5},{2,6},{3,7},{4,0},{5,1},{6,2},{7,3},{8,12},{9,13},{10,... | collective-permute-start | bytes 9142280 | tf_op jit(solution)/shard_map/ppermute | solution.py:344
  215.9 10.3 %collective-permute-start.23 = (bf16[384,768]{1,0:T(8,128)(2,1)}, bf16[384,768]{1,0:T(8,128)(2,1)}, u32[]{:S(2)}, u32[]{:S(2)}) collective-permute-start(bf16[384,768]{1,0:T(8,128)(2,1)} %fusion.12), channel_id=1, source_target_pairs={{0,8},{1,9},{2,10},{3,11},{4,20},{5,21},{6,22},{7,23},{8,0},{9,1},... | collective-permute-start | bytes 1769480 | tf_op jit(solution)/shard_map/ppermute | solution.py:349
  229.2 31.9 %collective-permute-start.25 = (bf16[2,96,3968]{2,1,0:T(8,128)(2,1)}, bf16[2,96,3968]{2,1,0:T(8,128)(2,1)}, u32[]{:S(2)}, u32[]{:S(2)}) collective-permute-start(bf16[2,96,3968]{2,1,0:T(8,128)(2,1)} %pad_maximum_fusion.2), channel_id=1, source_target_pairs={{0,16},{1,17},{2,18},{3,19},{4,12},{5,13},{6,14},{7,15},{8,24},{9,... | collective-permute-start | bytes 4571144 | tf_op jit(solution)/shard_map/ppermute | solution.py:349
  236.0 24.3 %collective-permute-start.38 = (bf16[96,768]{1,0:T(8,128)(2,1)S(1)}, bf16[96,768]{1,0:T(8,128)(2,1)S(1)}, u32[]{:S(2)}, u32[]{:S(2)}) collective-permute-start(bf16[96,768]{1,0:T(8,128)(2,1)S(1)} %get-tuple-element.142), channel_id=1, source_target_pairs={{0,3},{1,0},{2,1},{3,2},{4,7},{5,4},{6,5},{7,6},{8,11},{9,8},{10,9... | collective-permute-start | bytes 442376 | tf_op jit(solution)/shard_map/ppermute | solution.py:353
  239.2 21.1 %collective-permute-start.37 = (bf16[96,768]{1,0:T(8,128)(2,1)S(1)}, bf16[96,768]{1,0:T(8,128)(2,1)S(1)}, u32[]{:S(2)}, u32[]{:S(2)}) collective-permute-start(bf16[96,768]{1,0:T(8,128)(2,1)S(1)} %get-tuple-element.143), channel_id=1, source_target_pairs={{0,2},{1,3},{2,0},{3,1},{4,6},{5,7},{6,4},{7,5},{8,10},{9,11},{10,... | collective-permute-start | bytes 442376 | tf_op jit(solution)/shard_map/ppermute | solution.py:353
  242.1 18.1 %collective-permute-start.36 = (bf16[96,768]{1,0:T(8,128)(2,1)S(1)}, bf16[96,768]{1,0:T(8,128)(2,1)S(1)}, u32[]{:S(2)}, u32[]{:S(2)}) collective-permute-start(bf16[96,768]{1,0:T(8,128)(2,1)S(1)} %get-tuple-element.141), channel_id=1, source_target_pairs={{0,1},{1,2},{2,3},{3,0},{4,5},{5,6},{6,7},{7,4},{8,9},{9,10},{10,1... | collective-permute-start | bytes 442376 | tf_op jit(solution)/shard_map/ppermute | solution.py:353
  273.8 12.0 %collective-permute-start.32 = (bf16[96,3968]{1,0:T(8,128)(2,1)}, bf16[96,3968]{1,0:T(8,128)(2,1)}, u32[]{:S(2)}, u32[]{:S(2)}) collective-permute-start(bf16[96,3968]{1,0:T(8,128)(2,1)} %fusion.7), channel_id=1, source_target_pairs={{0,8},{1,9},{2,10},{3,11},{4,20},{5,21},{6,22},{7,23},{8,0},{9,1},... | collective-permute-start | bytes 2285576 | tf_op jit(solution)/shard_map/ppermute | solution.py:349
  276.6 14.1 %collective-permute-start.26 = (bf16[4,96,2304]{2,1,0:T(8,128)(2,1)}, bf16[4,96,2304]{2,1,0:T(8,128)(2,1)}, u32[]{:S(2)}, u32[]{:S(2)}) collective-permute-start(bf16[4,96,2304]{2,1,0:T(8,128)(2,1)} %dynamic-slice_bitcast_fusion.2), channel_id=1, source_target_pairs={{0,4},{1,5},{2,6},{3,7},{4,0},{5,1},{6,2},{7,3},{8,12},{9,13},{10,... | collective-permute-start | bytes 5308424 | tf_op jit(solution)/shard_map/ppermute | solution.py:344
  288.1 7.2 %collective-permute-start.35 = (bf16[24,3968]{1,0:T(8,128)(2,1)S(1)}, bf16[24,3968]{1,0:T(8,128)(2,1)S(1)}, u32[]{:S(2)}, u32[]{:S(2)}) collective-permute-start(bf16[24,3968]{1,0:T(8,128)(2,1)S(1)} %get-tuple-element.139), channel_id=1, source_target_pairs={{0,3},{1,0},{2,1},{3,2},{4,7},{5,4},{6,5},{7,6},{8,11},{9,8},{10,9... | collective-permute-start | bytes 571400 | tf_op jit(solution)/shard_map/ppermute | solution.py:353
  290.0 15.4 %collective-permute-start.34 = (bf16[24,3968]{1,0:T(8,128)(2,1)S(1)}, bf16[24,3968]{1,0:T(8,128)(2,1)S(1)}, u32[]{:S(2)}, u32[]{:S(2)}) collective-permute-start(bf16[24,3968]{1,0:T(8,128)(2,1)S(1)} %get-tuple-element.140), channel_id=1, source_target_pairs={{0,2},{1,3},{2,0},{3,1},{4,6},{5,7},{6,4},{7,5},{8,10},{9,11},{10,... | collective-permute-start | bytes 571400 | tf_op jit(solution)/shard_map/ppermute | solution.py:353
  290.0 15.4 %collective-permute-start.33 = (bf16[24,3968]{1,0:T(8,128)(2,1)S(1)}, bf16[24,3968]{1,0:T(8,128)(2,1)S(1)}, u32[]{:S(2)}, u32[]{:S(2)}) collective-permute-start(bf16[24,3968]{1,0:T(8,128)(2,1)S(1)} %get-tuple-element.138), channel_id=1, source_target_pairs={{0,1},{1,2},{2,3},{3,0},{4,5},{5,6},{6,7},{7,4},{8,9},{9,10},{10,1... | collective-permute-start | bytes 571400 | tf_op jit(solution)/shard_map/ppermute | solution.py:353
  292.3 16.4 %collective-permute-start.27 = (bf16[2,96,2304]{2,1,0:T(8,128)(2,1)S(1)}, bf16[2,96,2304]{2,1,0:T(8,128)(2,1)S(1)}, u32[]{:S(2)}, u32[]{:S(2)}) collective-permute-start(bf16[2,96,2304]{2,1,0:T(8,128)(2,1)S(1)} %pad_maximum_fusion.6), channel_id=1, source_target_pairs={{0,16},{1,17},{2,18},{3,19},{4,12},{5,13},{6,14},{7,15},{8,24},{9,... | collective-permute-start | bytes 2654216 | tf_op jit(solution)/shard_map/ppermute | solution.py:349
  310.8 14.0 %collective-permute-start.28 = (bf16[96,2304]{1,0:T(8,128)(2,1)}, bf16[96,2304]{1,0:T(8,128)(2,1)}, u32[]{:S(2)}, u32[]{:S(2)}) collective-permute-start(bf16[96,2304]{1,0:T(8,128)(2,1)} %fusion.15), channel_id=1, source_target_pairs={{0,8},{1,9},{2,10},{3,11},{4,20},{5,21},{6,22},{7,23},{8,0},{9,1},... | collective-permute-start | bytes 1327112 | tf_op jit(solution)/shard_map/ppermute | solution.py:349
  312.7 12.1 %all-to-all-start.1 = ((f32[32,1,1024]{2,1,0:T(1,128)}), f32[32,1,1024]{2,1,0:T(1,128)S(1)}, u32[]{:S(2)}, u32[]{:S(2)}) async-start(f32[32,1,1024]{2,1,0:T(1,128)} %all_to_all.14), calls=%async_computation.1 | async-start | bytes 262144 | tf_op jit(solution)/shard_map/all_to_all | solution.py:464
  326.4 6.8 %collective-permute-start.31 = (bf16[24,2304]{1,0:T(8,128)(2,1)S(1)}, bf16[24,2304]{1,0:T(8,128)(2,1)S(1)}, u32[]{:S(2)}, u32[]{:S(2)}) collective-permute-start(bf16[24,2304]{1,0:T(8,128)(2,1)S(1)} %get-tuple-element.149), channel_id=1, source_target_pairs={{0,3},{1,0},{2,1},{3,2},{4,7},{5,4},{6,5},{7,6},{8,11},{9,8},{10,9... | collective-permute-start | bytes 331784 | tf_op jit(solution)/shard_map/ppermute | solution.py:353
  327.6 10.6 %collective-permute-start.30 = (bf16[24,2304]{1,0:T(8,128)(2,1)S(1)}, bf16[24,2304]{1,0:T(8,128)(2,1)S(1)}, u32[]{:S(2)}, u32[]{:S(2)}) collective-permute-start(bf16[24,2304]{1,0:T(8,128)(2,1)S(1)} %get-tuple-element.150), channel_id=1, source_target_pairs={{0,2},{1,3},{2,0},{3,1},{4,6},{5,7},{6,4},{7,5},{8,10},{9,11},{10,... | collective-permute-start | bytes 331784 | tf_op jit(solution)/shard_map/ppermute | solution.py:353
  327.7 10.6 %collective-permute-start.29 = (bf16[24,2304]{1,0:T(8,128)(2,1)S(1)}, bf16[24,2304]{1,0:T(8,128)(2,1)S(1)}, u32[]{:S(2)}, u32[]{:S(2)}) collective-permute-start(bf16[24,2304]{1,0:T(8,128)(2,1)S(1)} %get-tuple-element.148), channel_id=1, source_target_pairs={{0,1},{1,2},{2,3},{3,0},{4,5},{5,6},{6,7},{7,4},{8,9},{9,10},{10,1... | collective-permute-start | bytes 331784 | tf_op jit(solution)/shard_map/ppermute | solution.py:353
  (65 other events, 529.5 us)
where the time goes:
time: 345 us; the launch traced here: 339 us
  waiting for transfers between devices  75.8 us (22%)
  Pallas kernels  60.7 us (18%)
  starting transfers between devices  56.9 us (16%)
  matrix products  52 us (15%)
  other arithmetic  50 us (14%)
  local copies, waits for them, and re-layouts  40.1 us (12%)
  between operations  3.95 us (1%)
    ppermute x12, waiting for transfers between devices, swap_chips(): lax.ppermute(array, AXES, [(i, i ^ masks[i // 4 % 2]) for i in range(32)])  46.6 us
    ppermute x18, starting transfers between devices, turn(): lax.ppermute(array, AXES, [(i, i // 4 * 4 + (i + step) % 4) for i in rang...  29.5 us
    dot_general x4, matrix products, dot_nt(): lax.dot_general(left, right, (((1,), (1,)), ((), ())), precision=precisio...  26.2 us
    ppermute x18, waiting for transfers between devices, turn(): lax.ppermute(array, AXES, [(i, i // 4 * 4 + (i + step) % 4) for i in rang...  25.6 us
    dot_general x4, matrix products, dot_tn(): lax.dot_general(left, right, (((0,), (0,)), ((), ())), precision=precisio...  16.7 us
    ppermute x12, starting transfers between devices, swap_chips(): lax.ppermute(array, AXES, [(i, i ^ masks[i // 4 % 2]) for i in range(32)])  16.3 us
    pallas_call x1, Pallas kernels, attend_back(): pl.pallas_call(functools.partial(attend_back_kernel, width), grid=(frames...  16.2 us
    pallas_call x1, Pallas kernels, widen(): pl.pallas_call(widen_kernel, grid=(hidden // cut,), in_specs=[pl.BlockSpe...  13.7 us
  transfers between devices with their start and end apart: 41, of which 12 were waited for; matrix products, arithmetic and copies ran while one was open for 24% of the time, Pallas kernels for 9%

commit v1 on v0

v1 whole, which is shorter than its diff:
```python
import functools
import math

import jax
import jax.numpy as jnp
from jax import lax
from jax.experimental import pallas as pl
from jax.experimental.pallas import tpu as pltpu
from jax.sharding import PartitionSpec as P

HEADS = 12
HDIM = 64
NTOK = 8
P_SIZE = 196
PAD = -(-P_SIZE // 16) * 16
LANES = 128
EPS = 1e-06
AXES = ("dp", "sub")
MIB = 1 << 20
SPEED = 4.0e9
LOW = jnp.bfloat16
WIDE = jnp.float32
exact_mode = lax.Precision.HIGHEST


def took(microseconds):
    return pl.CostEstimate(
        flops=int(microseconds * SPEED), bytes_accessed=0, transcendentals=0
    )


def dot_nn(left, right, precision=None):
    return lax.dot_general(
        left, right, (((1,), (0,)), ((), ())), precision=precision, preferred_element_type=WIDE
    )


def dot_nt(left, right, precision=None):
    return lax.dot_general(
        left, right, (((1,), (1,)), ((), ())), precision=precision, preferred_element_type=WIDE
    )


def dot_tn(left, right, precision=None):
    return lax.dot_general(
        left, right, (((0,), (0,)), ((), ())), precision=precision, preferred_element_type=WIDE
    )


def gelu_pair(v):
    phi = 0.5 + 0.5 * lax.erf(v * math.sqrt(0.5))
    bell = jnp.exp(-0.5 * v * v) * (1.0 / math.sqrt(2.0 * math.pi))
    return v * phi, phi + v * bell


def norm_parts(rows):
    center = rows - jnp.mean(rows, axis=-1, keepdims=True)
    scale = lax.rsqrt(jnp.mean(center * center, axis=-1, keepdims=True) + EPS)
    return center * scale, scale


def norm_back(unit, scale, gain, grad):
    inner = grad * gain
    return scale * (
        inner
        - jnp.mean(inner, axis=-1, keepdims=True)
        - unit * jnp.mean(inner * unit, axis=-1, keepdims=True)
    )


def key_rows_live():
    return lax.broadcasted_iota(jnp.int32, (PAD, PAD), 0) < P_SIZE


def of_head(pair, first):
    low_lanes = lax.broadcasted_iota(jnp.int32, pair.shape, 1) < HDIM
    return jnp.where(low_lanes == first, pair, jnp.zeros_like(pair))


def flip(block):
    return jnp.swapaxes(block.astype(WIDE), 0, 1)


def attend_kernel(*refs):
    groups = len(refs) - 2
    out_ref, log_ref = refs[groups:]
    live = key_rows_live()
    head = 0
    for qkv_ref in refs[:groups]:
        width = qkv_ref.shape[1] // 3
        for pair in range(width // LANES):
            q = qkv_ref[:, pair * LANES : (pair + 1) * LANES]
            k = qkv_ref[:, width + pair * LANES : width + (pair + 1) * LANES]
            v = qkv_ref[:, 2 * width + pair * LANES : 2 * width + (pair + 1) * LANES]
            v_flip = flip(v).astype(LOW)
            halves = []
            for half in range(2):
                scores = jnp.where(live, dot_nt(of_head(k, half == 0), q), -1e30)
                top = jnp.max(scores, axis=0, keepdims=True)
                power = jnp.exp(scores - top)
                total = jnp.sum(power, axis=0, keepdims=True)
                soft = (power * (1.0 / total)).astype(LOW)
                halves.append(dot_nn(v_flip[half * HDIM : (half + 1) * HDIM], soft))
                log_ref[0, head : head + 1, :] = top + jnp.log(total)
                head += 1
            out_ref[:, (head - 2) * HDIM : head * HDIM] = jnp.swapaxes(
                jnp.concatenate(halves, axis=0), 0, 1
            ).astype(LOW)


def attend(qkvs):
    frames = qkvs[0].shape[0] // PAD
    width = sum(qkv.shape[1] for qkv in qkvs) // 3
    return pl.pallas_call(
        attend_kernel,
        grid=(frames,),
        in_specs=[pl.BlockSpec((PAD, qkv.shape[1]), lambda f: (f, 0)) for qkv in qkvs],
        out_specs=[
            pl.BlockSpec((PAD, width), lambda f: (f, 0)),
            pl.BlockSpec((1, 16, PAD), lambda f: (f, 0, 0)),
        ],
        out_shape=[
            jax.ShapeDtypeStruct((frames * PAD, width), LOW),
            jax.ShapeDtypeStruct((frames, 16, PAD), WIDE),
        ],
        compiler_params=pltpu.CompilerParams(vmem_limit_bytes=24 * MIB),
        cost_estimate=took(11),
        name="attend",
    )(*qkvs)


def attend_back_kernel(first_head, qkv_ref, log_ref, grad_ref, out_ref, sum_ref):
    live = key_rows_live()
    width = qkv_ref.shape[1] // 3
    low_lanes = lax.broadcasted_iota(jnp.int32, (PAD, LANES), 1) < HDIM
    for pair in range(width // LANES):
        at_q = slice(pair * LANES, (pair + 1) * LANES)
        at_k = slice(width + pair * LANES, width + (pair + 1) * LANES)
        at_v = slice(2 * width + pair * LANES, 2 * width + (pair + 1) * LANES)
        q, k, v, grad = qkv_ref[:, at_q], qkv_ref[:, at_k], qkv_ref[:, at_v], grad_ref[:, at_q]
        k_flip = flip(k).astype(LOW)
        grads_q, grads_k, grads_v = [], [], []
        for half in range(2):
            head = first_head + 2 * pair + half
            scores = dot_nt(of_head(k, half == 0), q)
            soft = jnp.where(live, jnp.exp(scores - log_ref[0, head : head + 1, :]), 0.0)
            grads_v.append(dot_nn(soft.astype(LOW), grad))
            grad_soft = dot_nt(of_head(v, half == 0), grad)
            row = jnp.sum(grad_soft * soft, axis=0, keepdims=True)
            grad_scores = (soft * (grad_soft - row)).astype(LOW)
            grads_k.append(dot_nn(grad_scores, q))
            grads_q.append(dot_nn(k_flip[half * HDIM : (half + 1) * HDIM], grad_scores))
        grad_q = jnp.swapaxes(jnp.concatenate(grads_q, axis=0), 0, 1).astype(LOW)
        out_ref[:, at_q] = (grad_q.astype(WIDE) * 0.125).astype(LOW)
        out_ref[:, at_k] = jnp.where(low_lanes, grads_k[0], grads_k[1]).astype(LOW)
        out_ref[:, at_v] = jnp.where(low_lanes, grads_v[0], grads_v[1]).astype(LOW)

    @pl.when(pl.program_id(0) == 0)
    def _():
        sum_ref[...] = jnp.zeros_like(sum_ref)

    sum_ref[0:1, :] += jnp.sum(out_ref[...].astype(WIDE), axis=0, keepdims=True)


def attend_back(qkv, logs, grad, group):
    frames = qkv.shape[0] // PAD
    width = qkv.shape[1] // 3
    return pl.pallas_call(
        functools.partial(attend_back_kernel, group * width // HDIM),
        grid=(frames,),
        in_specs=[
            pl.BlockSpec((PAD, 3 * width), lambda f: (f, 0)),
            pl.BlockSpec((1, 16, PAD), lambda f: (f, 0, 0)),
            pl.BlockSpec((PAD, width), lambda f: (f, group)),
        ],
        out_specs=[
            pl.BlockSpec((PAD, 3 * width), lambda f: (f, 0)),
            pl.BlockSpec((8, 3 * width), lambda f: (0, 0)),
        ],
        out_shape=[
            jax.ShapeDtypeStruct(qkv.shape, LOW),
            jax.ShapeDtypeStruct((8, 3 * width), WIDE),
        ],
        compiler_params=pltpu.CompilerParams(vmem_limit_bytes=24 * MIB),
        cost_estimate=took(9.2),
        name="attend_back",
    )(qkv, logs, grad)


def widen_kernel(rows_ref, w_ref, b_ref, low_ref, slope_ref):
    act, slope = gelu_pair(dot_nn(rows_ref[...], w_ref[...]) + b_ref[...])
    low_ref[...] = act.astype(LOW)
    slope_ref[...] = slope.astype(LOW)


def widen(rows, w, b):
    count, width = rows.shape
    hidden = w.shape[1]
    cut = 512
    return pl.pallas_call(
        widen_kernel,
        grid=(hidden // cut,),
        in_specs=[
            pl.BlockSpec((count, width), lambda n: (0, 0)),
            pl.BlockSpec((width, cut), lambda n: (0, n)),
            pl.BlockSpec((1, cut), lambda n: (0, n)),
        ],
        out_specs=[pl.BlockSpec((count, cut), lambda n: (0, n))] * 2,
        out_shape=[jax.ShapeDtypeStruct((count, hidden), LOW)] * 2,
        compiler_params=pltpu.CompilerParams(vmem_limit_bytes=32 * MIB),
        cost_estimate=took(9.7),
        name="widen",
    )(rows, w, b)


def steep_kernel(grad_ref, w_ref, slope_ref, out_ref, sum_ref):
    out = (dot_nt(grad_ref[...], w_ref[...]) * slope_ref[...].astype(WIDE)).astype(LOW)
    out_ref[...] = out
    sum_ref[...] = jnp.sum(out.astype(WIDE), axis=0, keepdims=True)


def steep(grad, w, slope):
    count, width = grad.shape
    hidden = w.shape[0]
    cut = 384
    return pl.pallas_call(
        steep_kernel,
        grid=(hidden // cut,),
        in_specs=[
            pl.BlockSpec((count, width), lambda n: (0, 0)),
            pl.BlockSpec((cut, width), lambda n: (n, 0)),
            pl.BlockSpec((count, cut), lambda n: (0, n)),
        ],
        out_specs=[
            pl.BlockSpec((count, cut), lambda n: (0, n)),
            pl.BlockSpec((1, cut), lambda n: (0, n)),
        ],
        out_shape=[
            jax.ShapeDtypeStruct((count, hidden), LOW),
            jax.ShapeDtypeStruct((1, hidden), WIDE),
        ],
        compiler_params=pltpu.CompilerParams(vmem_limit_bytes=32 * MIB),
        cost_estimate=took(8.4),
        name="steep",
    )(grad, w, slope)


def learn_kernel(
    live_ref,
    count_ref,
    second_ref,
    cot_ref,
    gain_ref,
    bias_ref,
    w_one_ref,
    b_one_ref,
    w_two_ref,
    b_two_ref,
    pooled_ref,
    grad_ref,
    grad_low_ref,
    sums_ref,
    grad_one_ref,
    grad_two_ref,
    small_ref,
):
    frame = pl.program_id(0)
    live = jnp.where(frame < live_ref[0], 1.0, 0.0)
    pair_norm = P_SIZE * NTOK * (NTOK - 1)
    pull = live / (count_ref[...] * pair_norm)
    second = second_ref[...]
    gain = gain_ref[...]
    unit, scale = norm_parts(second)
    normed = (unit * gain + bias_ref[...]).astype(LOW)
    w_one = w_one_ref[...]
    act, slope = gelu_pair(dot_nn(normed, w_one) + b_one_ref[...])
    w_two = w_two_ref[...]
    logits = dot_nn(act, w_two, exact_mode) + b_two_ref[...]
    row = lax.broadcasted_iota(jnp.int32, (PAD, LANES), 0)
    lane = lax.broadcasted_iota(jnp.int32, (PAD, LANES), 1)
    inside = (row < P_SIZE) & (lane < NTOK)
    maps = jnp.where(inside, 1.0 / (1.0 + jnp.exp(-logits)), 0.0)
    maps_low = maps.astype(LOW)
    second_low = second.astype(LOW)
    pooled = dot_tn(maps_low, second_low)
    pooled_ref[...] = pooled[:NTOK] * (live / P_SIZE)
    column = jnp.sum(maps, axis=1, keepdims=True)
    crossing = jnp.sum(column * column) - jnp.sum(maps * maps)
    cot = jnp.concatenate([cot_ref[...], jnp.zeros((LANES - NTOK, cot_ref.shape[1]), WIDE)], axis=0)
    cot = cot.astype(LOW)
    grad_maps = dot_nt(second_low, cot) * (live / P_SIZE) + (2.0 * pull) * (column - maps)
    grad_logits = jnp.where(inside, grad_maps * maps * (1.0 - maps), 0.0)
    grad_learn = (dot_nt(grad_logits, w_two, exact_mode) * slope).astype(LOW)
    grad_normed = dot_nt(grad_learn, w_one)
    grad = norm_back(unit, scale, gain, grad_normed) + dot_nn(maps_low, cot) * (live / P_SIZE)
    grad_ref[...] = grad
    grad_low = grad.astype(LOW)
    grad_low_ref[...] = grad_low

    @pl.when(frame == 0)
    def _():
        sums_ref[...] = jnp.zeros_like(sums_ref)
        grad_one_ref[...] = jnp.zeros_like(grad_one_ref)
        grad_two_ref[...] = jnp.zeros_like(grad_two_ref)
        small_ref[...] = jnp.zeros_like(small_ref)

    sums_ref[0:1, :] += jnp.sum(grad_normed * unit, axis=0, keepdims=True)
    sums_ref[1:2, :] += jnp.sum(grad_normed, axis=0, keepdims=True)
    sums_ref[2:3, :] += jnp.sum(grad_low.astype(WIDE), axis=0, keepdims=True)
    grad_one_ref[...] += dot_tn(normed, grad_learn)
    grad_two_ref[...] += dot_tn(act, grad_logits, exact_mode)
    small_ref[0:1, :] += jnp.sum(grad_learn.astype(WIDE), axis=0, keepdims=True)
    small_ref[1:2, :] += jnp.sum(grad_logits, axis=0, keepdims=True)
    small_ref[2:3, :] += crossing * pull


def learn(live, count_live, second, cot, gain, bias, w_one, b_one, w_two, b_two):
    count, width = second.shape
    frames = count // PAD
    whole = lambda *shape: pl.BlockSpec(shape, lambda f, *_: (0,) * len(shape))
    rows = lambda high, wide: pl.BlockSpec((high, wide), lambda f, *_: (f, 0))
    return pl.pallas_call(
        learn_kernel,
        grid_spec=pltpu.PrefetchScalarGridSpec(
            num_scalar_prefetch=1,
            grid=(frames,),
            in_specs=[
                whole(1, LANES),
                rows(PAD, width),
                rows(NTOK, width),
                whole(1, width),
                whole(1, width),
                whole(width, LANES),
                whole(1, LANES),
                whole(LANES, LANES),
                whole(1, LANES),
            ],
            out_specs=[
                rows(NTOK, width),
                rows(PAD, width),
                rows(PAD, width),
                whole(8, width),
                whole(width, LANES),
                whole(LANES, LANES),
                whole(8, LANES),
            ],
        ),
        out_shape=[
            jax.ShapeDtypeStruct((frames * NTOK, width), WIDE),
            jax.ShapeDtypeStruct((count, width), WIDE),
            jax.ShapeDtypeStruct((count, width), LOW),
            jax.ShapeDtypeStruct((8, width), WIDE),
            jax.ShapeDtypeStruct((width, LANES), WIDE),
            jax.ShapeDtypeStruct((LANES, LANES), WIDE),
            jax.ShapeDtypeStruct((8, LANES), WIDE),
        ],
        compiler_params=pltpu.CompilerParams(vmem_limit_bytes=24 * MIB),
        cost_estimate=took(10.2),
        name="learn",
    )(live, count_live, second, cot, gain, bias, w_one, b_one, w_two, b_two)


def ease_two_kernel(
    grad_ref,
    w_ref,
    first_ref,
    gain_ref,
    second_ref,
    w_out_ref,
    out_ref,
    low_ref,
    attended_ref,
    sums_ref,
):
    grad = dot_nt(grad_ref[...], w_ref[...])
    unit, scale = norm_parts(first_ref[...])
    out = second_ref[...] + norm_back(unit, scale, gain_ref[...], grad)
    out_ref[...] = out
    low = out.astype(LOW)
    low_ref[...] = low
    attended_ref[...] = dot_nt(low, w_out_ref[...]).astype(LOW)

    @pl.when(pl.program_id(0) == 0)
    def _():
        sums_ref[...] = jnp.zeros_like(sums_ref)

    sums_ref[0:1, :] += jnp.sum(grad * unit, axis=0, keepdims=True)
    sums_ref[1:2, :] += jnp.sum(grad, axis=0, keepdims=True)
    sums_ref[2:3, :] += jnp.sum(low.astype(WIDE), axis=0, keepdims=True)


def ease_two(grad, w, first, gain, second, w_out):
    count, width = first.shape
    hidden = w.shape[1]
    some = count // 2
    rows = lambda wide: pl.BlockSpec((some, wide), lambda f: (f, 0))
    whole = lambda *shape: pl.BlockSpec(shape, lambda f: (0, 0))
    return pl.pallas_call(
        ease_two_kernel,
        grid=(count // some,),
        in_specs=[
            rows(hidden),
            whole(width, hidden),
            rows(width),
            whole(1, width),
            rows(width),
            whole(width, width),
        ],
        out_specs=[rows(width), rows(width), rows(width), whole(8, width)],
        out_shape=[
            jax.ShapeDtypeStruct((count, width), WIDE),
            jax.ShapeDtypeStruct((count, width), LOW),
            jax.ShapeDtypeStruct((count, width), LOW),
            jax.ShapeDtypeStruct((8, width), WIDE),
        ],
        compiler_params=pltpu.CompilerParams(vmem_limit_bytes=40 * MIB),
        cost_estimate=took(12),
        name="ease_two",
    )(grad, w, first, gain, second, w_out)


def ease_one_kernel(groups, *refs):
    grads, weights = refs[:groups], refs[groups : 2 * groups]
    rows_ref, gain_ref, first_ref, out_ref, sums_ref = refs[2 * groups :]
    grad = sum(dot_nt(g[...], w[...]) for g, w in zip(grads, weights))
    unit, scale = norm_parts(rows_ref[...].astype(WIDE))
    out = first_ref[...] + norm_back(unit, scale, gain_ref[...], grad)
    out_ref[0] = out[:P_SIZE]

    @pl.when(pl.program_id(0) == 0)
    def _():
        sums_ref[...] = jnp.zeros_like(sums_ref)

    sums_ref[0:1, :] += jnp.sum(grad * unit, axis=0, keepdims=True)
    sums_ref[1:2, :] += jnp.sum(grad, axis=0, keepdims=True)


def ease_one(grads, weights, inputs, gain, first):
    count, width = first.shape
    frames = count // PAD
    rows = lambda wide: pl.BlockSpec((PAD, wide), lambda f: (f, 0))
    whole = lambda *shape: pl.BlockSpec(shape, lambda f: (0, 0))
    return pl.pallas_call(
        functools.partial(ease_one_kernel, len(grads)),
        grid=(frames,),
        in_specs=[rows(g.shape[1]) for g in grads]
        + [whole(*w.shape) for w in weights]
        + [rows(width), whole(1, width), rows(width)],
        out_specs=[
            pl.BlockSpec((1, P_SIZE, width), lambda f: (f, 0, 0)),
            whole(8, width),
        ],
        out_shape=[
            jax.ShapeDtypeStruct((frames, P_SIZE, width), WIDE),
            jax.ShapeDtypeStruct((8, width), WIDE),
        ],
        compiler_params=pltpu.CompilerParams(vmem_limit_bytes=40 * MIB),
        cost_estimate=took(6.3),
        name="ease_one",
    )(*grads, *weights, inputs, gain, first)


def places():
    dp = lax.axis_index("dp")
    return dp % 2, dp // 2, lax.axis_index("sub")


def swap_cores(array):
    return lax.ppermute(array, AXES, [(i, i ^ 4) for i in range(32)])


def swap_chips(array, first):
    masks = (8, 16) if first else (16, 8)
    return lax.ppermute(array, AXES, [(i, i ^ masks[i // 4 % 2]) for i in range(32)])


def turn(array, step):
    return lax.ppermute(array, AXES, [(i, i // 4 * 4 + (i + step) % 4) for i in range(32)])


def tie(*arrays):
    return lax.optimization_barrier(arrays)


def pack_kernel(slots, qkv_ref, out_ref, learn_ref, *refs):
    vector_refs, whole_ref, rows_ref = refs[:-2], refs[-2], refs[-1]
    wide, width, narrow = qkv_ref.shape[1], out_ref.shape[1], learn_ref.shape[1]
    whole_ref[:, :wide] = qkv_ref[...]
    whole_ref[:, wide : wide + width] = out_ref[...]
    whole_ref[:, wide + width : wide + width + LANES] = jnp.concatenate(
        [learn_ref[...], jnp.zeros((learn_ref.shape[0], LANES - narrow), LOW)], axis=1
    )
    if slots:
        rows_ref[...] = jnp.zeros_like(rows_ref)
        for (at, size), ref in zip(slots, vector_refs):
            line = at // LANES
            rows_ref[line : line + 1, at % LANES : at % LANES + size] = ref[...].astype(WIDE)[None]
        whole_ref[:, wide + width + LANES :] = rows_ref[...].astype(LOW)


def pack(w_qkv, w_out, w_learn, slots, vectors):
    high = w_out.shape[0]
    wide = w_qkv.shape[1] + w_out.shape[1] + (2 * LANES if slots else LANES)
    return pl.pallas_call(
        functools.partial(pack_kernel, slots),
        out_shape=jax.ShapeDtypeStruct((high, wide), LOW),
        scratch_shapes=[pltpu.VMEM((high, LANES), WIDE)],
        cost_estimate=took(1.7),
        name="pack",
    )(w_qkv, w_out, w_learn, *vectors)


def lay_kernel(cuts, at_ref, *refs):
    sources, wholes, sem = refs[:8], refs[8 : 8 + len(cuts)], refs[-1]
    chip, core = at_ref[0], at_ref[1]
    copies = []
    for n, source in enumerate(sources):
        side = core ^ (n // 4)
        place = (chip ^ (n % 2 * (1 + side) + n // 2 % 2 * (2 - side))) * 2 + side
        for whole, pieces in zip(wholes, cuts):
            at = 0
            for start, size in pieces:
                copies.append(
                    pltpu.make_async_copy(
                        source.at[:, pl.ds(start, size)],
                        whole.at[place, :, pl.ds(at, size)],
                        sem.at[len(copies)],
                    )
                )
                at += size
    for copy in copies:
        copy.start()
    for copy in copies:
        copy.wait()


def lay(sources, cuts):
    core, chip, _ = places()
    at = jnp.stack([chip, core]).astype(jnp.int32)
    shapes = [(8, sources[0].shape[0], sum(size for _, size in pieces)) for pieces in cuts]
    wholes = pl.pallas_call(
        functools.partial(lay_kernel, cuts),
        grid_spec=pltpu.PrefetchScalarGridSpec(
            num_scalar_prefetch=1,
            grid=(1,),
            in_specs=[pl.BlockSpec(memory_space=pl.ANY)] * 8,
            out_specs=[pl.BlockSpec(shape, lambda *_: (0, 0, 0)) for shape in shapes],
            scratch_shapes=[pltpu.SemaphoreType.DMA((8 * sum(map(len, cuts)),))],
        ),
        out_shape=[jax.ShapeDtypeStruct(shape, LOW) for shape in shapes],
        compiler_params=pltpu.CompilerParams(vmem_limit_bytes=24 * MIB),
        cost_estimate=took(3),
        name="lay",
    )(at, *sources)
    return [whole.reshape(-1, whole.shape[-1]) for whole in wholes]


def along_z(shard):
    return [shard] + [turn(shard, step) for step in (1, 2, 3)]


def join_z(parts):
    z = lax.axis_index("sub")
    return jnp.concatenate([lax.select_n((z - place) % 4, *parts) for place in range(4)], axis=0)


def block_order():
    core, chip, _ = places()
    first, second = 2 - core, 1 + core
    other = [(chip ^ off) * 2 + 1 - core for off in (0, first, second, 3)]
    own = [(chip ^ off) * 2 + core for off in (0, second, first, 3)]
    return jnp.stack(other + own).astype(jnp.int32)


def tall_kernel(order_ref, left_ref, right_ref, other_ref, own_ref):
    step = pl.program_id(0)
    block = dot_tn(left_ref[...], right_ref[...]).astype(LOW)

    @pl.when(step < 4)
    def _():
        other_ref[0] = block

    @pl.when(step >= 4)
    def _():
        own_ref[0] = block


def tall_grad(order, left, right):
    count, high = left.shape
    wide = right.shape[1]
    block = high // 8
    return pl.pallas_call(
        tall_kernel,
        grid_spec=pltpu.PrefetchScalarGridSpec(
            num_scalar_prefetch=1,
            grid=(8,),
            in_specs=[
                pl.BlockSpec((count, block), lambda n, order: (0, order[n])),
                pl.BlockSpec((count, wide), lambda n, order: (0, 0)),
            ],
            out_specs=[
                pl.BlockSpec((1, block, wide), lambda n, order: (jnp.minimum(n, 3), 0, 0)),
                pl.BlockSpec((1, block, wide), lambda n, order: (jnp.maximum(n - 4, 0), 0, 0)),
            ],
        ),
        out_shape=[jax.ShapeDtypeStruct((4, block, wide), LOW)] * 2,
        compiler_params=pltpu.CompilerParams(vmem_limit_bytes=32 * MIB),
        cost_estimate=took(8.4),
        name="tall_grad",
    )(order, left, right)


def wide_kernel(steps, order_ref, *refs):
    pairs = len(steps)
    lefts, rights = refs[:pairs], refs[pairs : 2 * pairs]
    other_ref, own_ref, turned_ref, blocks_ref = refs[2 * pairs :]
    step = pl.program_id(0)
    for n, start in enumerate(steps):

        @pl.when(step == start)
        def _():
            turned_ref[...] = flip(lefts[n][...]).astype(LOW)

        last = steps[n + 1] if n + 1 < pairs else pl.num_programs(0)

        @pl.when((step >= start) & (step < last))
        def _():
            block = dot_nn(turned_ref[...], rights[n][...])
            blocks_ref[...] = block.astype(LOW).reshape(blocks_ref.shape)

    for slot in range(4):
        other_ref[slot] = blocks_ref[order_ref[slot]]
        own_ref[slot] = blocks_ref[order_ref[4 + slot]]


def wide_grad(order, pairs, cut):
    count, high = pairs[0][0].shape
    steps, total = [], 0
    for _, right in pairs:
        steps.append(total)
        total += right.shape[1] // cut

    def right_spec(n):
        start, number = steps[n], pairs[n][1].shape[1] // cut
        return pl.BlockSpec(
            (count, cut), lambda i, order: (0, jnp.clip(i - start, 0, number - 1))
        )

    return pl.pallas_call(
        functools.partial(wide_kernel, steps),
        grid_spec=pltpu.PrefetchScalarGridSpec(
            num_scalar_prefetch=1,
            grid=(total,),
            in_specs=[pl.BlockSpec((count, high), lambda i, order: (0, 0))] * len(pairs)
            + [right_spec(n) for n in range(len(pairs))],
            out_specs=[pl.BlockSpec((4, high // 8, cut), lambda i, order: (0, 0, i))] * 2,
            scratch_shapes=[pltpu.VMEM((high, count), LOW), pltpu.VMEM((8, high // 8, cut), LOW)],
        ),
        out_shape=[jax.ShapeDtypeStruct((4, high // 8, total * cut), LOW)] * 2,
        compiler_params=pltpu.CompilerParams(vmem_limit_bytes=32 * MIB),
        cost_estimate=took(1.0 + 0.0024 * total * cut),
        name="wide_grad",
    )(order, *[left for left, _ in pairs], *[right for _, right in pairs])


class Sum:
    def __init__(self, other, own):
        self.other, self.own = other, own

    def to_core(self):
        self.from_core = swap_cores(self.other)

    def both(self, slot):
        return self.own[slot].astype(WIDE) + self.from_core[slot].astype(WIDE)

    def to_far(self):
        self.from_far = swap_chips(self.both(3).astype(LOW), False)

    def to_near(self):
        self.from_near = swap_chips(self.both(2).astype(LOW), False)

    def to_last(self):
        self.from_last = swap_chips((self.both(1) + self.from_far.astype(WIDE)).astype(LOW), True)

    def to_z(self):
        z = lax.axis_index("sub")
        layer = self.both(0) + self.from_near.astype(WIDE) + self.from_last.astype(WIDE)
        layer = layer.reshape((4, layer.shape[0] // 4) + layer.shape[1:])
        at = lambda step: lax.dynamic_index_in_dim(layer, (z + step) % 4, 0, False)
        self.layer = at(0)
        self.from_z = [turn(at(step).astype(LOW), step) for step in (1, 2, 3)]

    def total(self):
        return self.layer + sum(part.astype(WIDE) for part in self.from_z)


def after(value, *waits):
    parts = [getattr(one, name) for one, name in waits]
    value, *parts = tie(value, *parts)
    for (one, name), part in zip(waits, parts):
        setattr(one, name, part)
    return value


def exchange(rows):
    return lax.all_to_all(rows, AXES, 0, 0, tiled=True)


def slots_of(sizes):
    slots, at = [], 0
    for size in sizes:
        if at // LANES != (at + size - 1) // LANES:
            at = -(-at // LANES) * LANES
        slots.append((at, size))
        at += size
    return slots


def owners(size, at):
    lane = lax.broadcasted_iota(jnp.int32, (1, 32 * size), 1)
    owner = jnp.floor((lane.astype(WIDE) + 0.5) * (1.0 / size)).astype(jnp.int32)
    place = lane - owner * size + at % LANES
    pick = lax.broadcasted_iota(jnp.int32, (LANES, 32 * size), 0) == place
    mine = lax.broadcasted_iota(jnp.int32, (32, 32 * size), 0) == owner
    return jnp.where(pick, 1.0, 0.0).astype(LOW), mine


def unfold_kernel(slots, rows_ref, *refs):
    rows = rows_ref[...].astype(WIDE)
    out_refs, count_ref = refs[:-1], refs[-1]
    for (at, size), out_ref in zip(slots, out_refs):
        pick, mine = owners(size, at)
        spread = dot_nn(rows[:, at // LANES, :].astype(LOW), pick)
        out_ref[...] = jnp.sum(jnp.where(mine, spread, 0.0), axis=0, keepdims=True)
    at = slots[-1][0]
    count = jnp.sum(rows[:, at // LANES, at % LANES : at % LANES + 1])
    count_ref[...] = jnp.zeros_like(count_ref) + count


def unfold(slots, rows):
    return pl.pallas_call(
        functools.partial(unfold_kernel, slots),
        out_shape=[jax.ShapeDtypeStruct((1, 32 * size), WIDE) for _, size in slots[:-1]]
        + [jax.ShapeDtypeStruct((1, LANES), WIDE)],
        cost_estimate=took(2.4),
        name="unfold",
    )(rows.reshape(32, -1, LANES))


def fold_slabs(slots, vectors, slabs):
    out = [jnp.zeros((32, LANES), WIDE) for _ in range(slabs)]
    for (at, size), vector in zip(slots, vectors):
        pick, mine = owners(size, at)
        rest = jnp.where(mine, vector, 0.0)
        for _ in range(3):
            part = rest.astype(LOW)
            out[at // LANES] += dot_nt(part, pick)
            rest = rest - part.astype(WIDE)
    return out


def payload_kernel(
    slots,
    pieces,
    three_ref,
    two_ref,
    one_ref,
    in_ref,
    *refs,
):
    qkv_refs = refs[: len(pieces)]
    learn_ref, head_ref, small_ref, out_ref = refs[len(pieces) :]
    qkv = [
        ref[0:1, part * size : (part + 1) * size]
        for part in (0, 2)
        for ref, size in zip(qkv_refs, pieces)
    ]
    vectors = (
        [one_ref[0:1, :], one_ref[1:2, :], jnp.concatenate(qkv, axis=1)]
        + [two_ref[2:3, :], two_ref[0:1, :], two_ref[1:2, :], in_ref[...]]
        + [three_ref[2:3, :], three_ref[0:1, :], three_ref[1:2, :]]
    )
    half = LANES // 2
    out_ref[:, 16:, :] = jnp.zeros((32, 8, LANES), WIDE)
    out_ref[:, :8, :] = jnp.concatenate(
        [learn_ref[:, :8, :half], learn_ref[:, 8:16, :half]], axis=2
    )
    head = jnp.swapaxes(head_ref[...], 0, 1)[:8, :half]
    out_ref[:, 8:16, :] = jnp.concatenate(
        [learn_ref[:, 16:, :half], jnp.broadcast_to(head[None], (32, 8, half))], axis=2
    )
    for n, slab in enumerate(fold_slabs(slots, vectors, 4)):
        out_ref[:, 16 + n, :] = slab
    lane = lax.broadcasted_iota(jnp.int32, (1, LANES), 1)
    last = jnp.where(lane < half, small_ref[0:1, :], pltpu.roll(small_ref[1:2, :], half, 1))
    last = jnp.where(lane < half + NTOK, last, small_ref[2:3, :])
    out_ref[:, 20, :] = jnp.broadcast_to(last, (32, LANES))


def totals_kernel(slots, table_ref, *refs):
    total = jnp.sum(table_ref[...], axis=0)
    half = LANES // 2
    vector_refs, (learn_ref, one_ref, head_ref, two_ref, last_ref) = refs[:-5], refs[-5:]
    for (at, size), ref in zip(slots, vector_refs):
        ref[...] = total[16 + at // LANES, at % LANES : at % LANES + size]
    learn_ref[:8, :] = total[:8, :half]
    learn_ref[8:16, :] = total[:8, half:]
    learn_ref[16:, :] = total[8:16, :half]
    head_ref[...] = jnp.swapaxes(total[8:16, half:], 0, 1)
    one_ref[...] = total[20, :half]
    two_ref[...] = total[20, half : half + NTOK]
    last_ref[...] = total[20, half + NTOK : half + NTOK + 1]


def columns_of(array, pieces):
    return jnp.concatenate([array[..., start : start + size] for start, size in pieces], axis=-1)


def pad_frames(rows):
    frames = rows.shape[0] // P_SIZE
    rows = rows.reshape(frames, P_SIZE, rows.shape[1])
    return jnp.pad(rows, ((0, 0), (0, PAD - P_SIZE), (0, 0))).reshape(frames * PAD, -1)


def local(
    quick,
    tokens,
    frames_live,
    cotangent,
    ln1_gain,
    ln1_bias,
    w_qkv,
    b_qv,
    w_out,
    b_out,
    ln2_gain,
    ln2_bias,
    w_in,
    b_in,
    w_back,
    b_back,
    ln3_gain,
    ln3_bias,
    tl_w1,
    tl_b1,
    tl_w2,
    tl_b2,
):
    width, hidden = tokens.shape[1], w_in.shape[1]
    frames = tokens.shape[0] // P_SIZE
    learn_wide = tl_w1.shape[1]
    row = lambda v: v.astype(WIDE)[None, :]
    lanes = lambda a: jnp.pad(a, [(0, 0)] * (a.ndim - 1) + [(0, LANES - a.shape[-1])])
    some = width // 2
    groups = [[(part * width + n * some, some) for part in range(3)] for n in range(2)]
    cuts = groups + [[(3 * width, width)], [(4 * width, LANES)]]
    vectors = (ln1_gain, ln1_bias, b_qv, b_out, ln2_gain, ln2_bias, b_in, b_back)
    vectors += (ln3_gain, ln3_bias)
    if quick:
        slots = slots_of([v.shape[0] for v in vectors] + [1])
        cuts = cuts + [[(4 * width + LANES, LANES)]]
        first = pack(w_qkv, w_out, tl_w1, slots, (*vectors, frames_live))
        line_one, line_in = along_z(first), along_z(w_in)
        layer_one = join_z(line_one)
        one_first, one_second = swap_chips(layer_one, True), swap_chips(layer_one, False)
        one_first, *line_in = tie(one_first, *line_in)
        layer_in = join_z(line_in)
        line_back = along_z(tie(w_back, layer_in)[0])
        one_third = swap_chips(one_first, False)
        in_first, in_second = swap_chips(layer_in, True), swap_chips(layer_in, False)
        one_third, one_second, in_first, *line_back = tie(
            one_third, one_second, in_first, *line_back
        )
        in_third = swap_chips(in_first, False)
        layer_back = join_z(line_back)
        back_first, back_second = swap_chips(layer_back, True), swap_chips(layer_back, False)
        one_parts = [layer_one, one_first, one_second, one_third]
        one_whole = lay(one_parts + [swap_cores(part) for part in one_parts], cuts)
        *qkv_full, out_full, learn_full, vector_rows = one_whole
        *vectors, live_count = unfold(slots, vector_rows)
    else:
        every = lambda w: lax.all_gather(w, AXES, axis=0, tiled=True)
        first = pack(w_qkv, w_out, tl_w1, (), ())
        first_full, in_full, back_full = every(first), every(w_in), every(w_back)
        vectors = [every(v).astype(WIDE)[None, :] for v in vectors]
        live_count = jnp.zeros((1, LANES), WIDE) + jnp.sum(every(frames_live).astype(WIDE))
        *qkv_full, out_full, learn_full = [columns_of(first_full, pieces) for pieces in cuts]
    gain_one, bias_one, qkv_bias, out_bias, gain_two, bias_two, in_bias, back_bias = vectors[:8]
    gain_three, bias_three = vectors[8:]
    tokens_padded = pad_frames(tokens)
    inputs = tokens_padded.astype(WIDE)
    unit_one, scale_one = norm_parts(inputs)
    normed_one = (unit_one * gain_one + bias_one).astype(LOW)
    qkv_shift = jnp.concatenate(
        [qkv_bias[:, :width], jnp.zeros((1, width), WIDE), qkv_bias[:, width:]], axis=1
    )
    qkv_scale = jnp.concatenate([jnp.full(width, 0.125, WIDE), jnp.ones(2 * width, WIDE)])
    qkvs = []
    for pieces, weight in zip(groups, qkv_full):
        shift, scale = columns_of(qkv_shift, pieces), columns_of(qkv_scale, pieces)
        qkvs.append(((dot_nn(normed_one, weight) + shift) * scale).astype(LOW))
    attended, logs = attend(qkvs)
    residual_one = inputs + dot_nn(attended, out_full) + out_bias
    unit_two, scale_two = norm_parts(residual_one)
    normed_two = (unit_two * gain_two + bias_two).astype(LOW)
    if quick:
        normed_two, in_second, in_third, back_first = tie(
            normed_two, in_second, in_third, back_first
        )
        back_third = swap_chips(back_first, False)
        in_parts = [layer_in, in_first, in_second, in_third]
        (in_full,) = lay(in_parts + [swap_cores(part) for part in in_parts], [[(0, hidden)]])
    hidden_low, slope = widen(normed_two, in_full, in_bias)
    if quick:
        hidden_low, back_second, back_third = tie(hidden_low, back_second, back_third)
        back_parts = [layer_back, back_first, back_second, back_third]
        (back_full,) = lay(back_parts + [swap_cores(part) for part in back_parts], [[(0, width)]])
    residual_two = residual_one + dot_nn(hidden_low, back_full) + back_bias
    w_two = jnp.pad(lanes(tl_w2.astype(WIDE)), ((0, LANES - learn_wide), (0, 0)))
    pooled, grad_second, branch_two, sums_three, grad_learn_full, grad_head, small = learn(
        frames_live,
        live_count,
        residual_two,
        cotangent.astype(WIDE),
        gain_three,
        bias_three,
        learn_full,
        lanes(row(tl_b1)),
        w_two,
        lanes(row(tl_b2)),
    )
    if quick:
        order = block_order()
        sum_back = Sum(*tall_grad(order, hidden_low, branch_two))
        sum_back.to_core()
        branch_two = after(branch_two, (sum_back, "own"))
    grad_hidden, grad_in_bias = steep(branch_two, back_full, slope)
    if quick:
        grad_hidden = after(grad_hidden, (sum_back, "from_core"))
        sum_back.to_far()
        sum_in = Sum(*wide_grad(order, [(normed_two, grad_hidden)], width))
        sum_in.to_core()
        grad_hidden = after(grad_hidden, (sum_back, "from_far"), (sum_in, "own"))
        sum_back.to_last()
        sum_back.to_near()
    grad_first, branch_one, grad_attended, sums_two = ease_two(
        grad_hidden, in_full, residual_one, gain_two, grad_second, out_full
    )
    if quick:
        grad_attended = after(
            grad_attended, (sum_in, "from_core"), (sum_back, "from_last"), (sum_back, "from_near")
        )
        sum_in.to_far()
        sum_back.to_z()
    grad_one, sum_one = attend_back(qkvs[0], logs, grad_attended, 0)
    if quick:
        grad_one = after(grad_one, (sum_in, "from_far"), (sum_back, "from_z"))
        sum_in.to_last()
        sum_in.to_near()
        ones = [(normed_one, grad_one), (attended, branch_one)]
        sum_some = Sum(*wide_grad(order, ones, some))
        sum_some.to_core()
        grad_attended = after(grad_attended, (sum_some, "own"))
    grad_two, sum_two = attend_back(qkvs[1], logs, grad_attended, 1)
    grads, grads_qkv_bias = [grad_one, grad_two], [sum_one, sum_two]
    if quick:
        grad_two = after(
            grad_two, (sum_some, "from_core"), (sum_in, "from_last"), (sum_in, "from_near")
        )
        sum_some.to_far()
        sum_rest = Sum(*wide_grad(order, [(normed_one, grad_two)], some))
        sum_rest.to_core()
        grads[0] = after(grads[0], (sum_rest, "own"), (sum_some, "from_far"))
        sum_some.to_last()
        sum_some.to_near()
        sum_in.to_z()
    grad_tokens, sums_one = ease_one(grads, qkv_full, tokens_padded, gain_one, grad_first)
    if quick:
        sums_one = after(sums_one, (sum_rest, "from_core"), (sum_in, "from_z"))
        sum_rest.to_far()
    grad_tokens = grad_tokens.reshape(-1, width)
    if quick:
        slots = slots[:-1]
        payload = pl.pallas_call(
            functools.partial(payload_kernel, slots, (some,) * 2),
            out_shape=jax.ShapeDtypeStruct((32, 24, LANES), WIDE),
            cost_estimate=took(4.7),
            name="payload",
        )(
            *(sums_three, sums_two, sums_one, grad_in_bias),
            *grads_qkv_bias,
            *(grad_learn_full.reshape(32, -1, LANES), grad_head, small),
        )
        table = exchange(payload)
        payload = after(
            payload, (sum_rest, "from_far"), (sum_some, "from_last"), (sum_some, "from_near")
        )
        sum_rest.to_last()
        sum_rest.to_near()
        sum_some.to_z()
        sum_rest.to_z()
        back_rows, in_rows = sum_back.total(), sum_in.total()
        some_rows, rest_rows = sum_some.total(), sum_rest.total()
        out_rows = some_rows[:, 3 * some :]
        qkv_rows = [some_rows, rest_rows]
        *slices, learn_rows, learn_bias, head_rows, head_bias, penalty = pl.pallas_call(
            functools.partial(totals_kernel, slots),
            out_shape=[
                jax.ShapeDtypeStruct(shape, WIDE)
                for shape in [(size,) for _, size in slots]
                + [(width // 32, learn_wide), (learn_wide,), (learn_wide, NTOK), (NTOK,), (1,)]
            ],
            cost_estimate=took(1.5),
            name="totals",
        )(table)
        copied = (learn_bias, head_rows, head_bias, penalty[0])
    else:
        scatter = lambda a: lax.psum_scatter(a, AXES, scatter_dimension=0, tiled=True)
        back_rows = scatter(dot_tn(hidden_low, branch_two))
        qkv_rows = [scatter(dot_tn(normed_one, grad)) for grad in grads]
        out_rows = scatter(dot_tn(attended, branch_one))
        in_rows = scatter(dot_tn(normed_two, grad_hidden))
        learn_rows = scatter(grad_learn_full[:, :learn_wide])
        parts = [
            bias[0, part * some : (part + 1) * some] for part in (0, 2) for bias in grads_qkv_bias
        ]
        slices = [
            scatter(v)
            for v in (sums_one[0], sums_one[1], jnp.concatenate(parts), sums_two[2], sums_two[0])
            + (sums_two[1], grad_in_bias[0], sums_three[2], sums_three[0], sums_three[1])
        ]
        copied = lax.psum(
            (
                small[0, :learn_wide],
                grad_head[:learn_wide, :NTOK],
                small[1, :NTOK],
                small[2, 0],
            ),
            AXES,
        )
    parts = [rows[:, n * some : (n + 1) * some] for n in range(3) for rows in qkv_rows]
    return (
        pooled.astype(LOW),
        grad_tokens,
        slices[0],
        slices[1],
        jnp.concatenate(parts, axis=1),
        slices[2],
        out_rows,
        slices[3],
        slices[4],
        slices[5],
        in_rows,
        slices[6],
        back_rows,
        slices[7],
        slices[8],
        slices[9],
        learn_rows,
        copied[0],
        copied[1],
        copied[2],
        copied[3],
    )


def solution(mesh):
    quick = dict(mesh.shape) == {"dp": 8, "sub": 4}
    both = P(AXES)
    both_rows = P(AXES, None)
    copied = P()
    return jax.shard_map(
        functools.partial(local, quick),
        mesh=mesh,
        in_specs=(both_rows, both, both_rows, both, both, both_rows, both, both_rows)
        + (both, both, both, both_rows, both, both_rows, both, both, both, both_rows)
        + (copied, copied, copied),
        out_specs=(both_rows, both_rows, both, both, both_rows, both, both_rows)
        + (both, both, both, both_rows, both, both_rows, both, both, both, both_rows)
        + (copied, copied, copied, copied),
        check_vma=False,
    )
```

time: 345 us -> 303 us (0.88)
  Pallas kernels: 60.7 us -> 122 us
  matrix products: 52 us -> 9.13 us
  waiting for transfers between devices: 75.8 us -> 37.1 us
  other arithmetic: 50 us -> 26.6 us
  starting transfers between devices: 56.9 us -> 71.4 us
  local copies, waits for them, and re-layouts: 40.1 us -> 29.2 us
    pallas_call x2 -> x14, Pallas kernels: 27.2 us -> 95.4 us  [the longest x3 19.7 us: wide_grad(): pl.pallas_call(functools.partial(wide_kernel, steps), grid_spec=pltpu.Pre...]
    dot_general x8 -> x0, matrix products: 42.8 us -> none  [the longest x4 26.2 us: dot_nt(): lax.dot_general(left, right, (((1,), (1,)), ((), ())), precision=precisio...]
    ppermute x12 -> x21, waiting for transfers between devices: 46.6 us -> 5.37 us  [swap_chips(): lax.ppermute(array, AXES, [(i, i ^ masks[i // 4 % 2]) for i in range(32)])]
    unnamed x147 -> x149, local copies, waits for them, and re-layouts: 3.24 us -> 20.4 us
    ppermute x18 -> x21, starting transfers between devices: 29.5 us -> 43 us  [turn(): lax.ppermute(array, AXES, [(i, i // 4 * 4 + (i + step) % 4) for i in rang...]
    convert_element_type x8, other arithmetic: 17.3 us -> 6.96 us  [the longest x4 4.19 us: to_last(): (self.both(1) + self.from_far.astype(WIDE)).astype(LOW)]
    concatenate x4 -> x2, local copies, waits for them, and re-layouts: 9.64 us -> 0.61 us  [the longest x1 0.61 us: columns_of(): jnp.concatenate([array[..., start:start + size] for start, size in pieces...]
    squeeze x10 -> x0, local copies, waits for them, and re-layouts: 7.57 us -> none  [the longest x3 4.46 us: own(): at(at(p, self.chip ^ off, 0, False), self.core, 0, False)]
  transfers between devices with their start and end apart: 41 -> 59, of which waited for: 12 -> 13; matrix products, arithmetic and copies ran while one was open for 24% -> 12% of each run, Pallas kernels for 9% -> 31%
where the time goes in v1:
time: 303 us; the launch traced here: 298 us
  Pallas kernels  122 us (40%)
  starting transfers between devices  71.4 us (24%)
  waiting for transfers between devices  37.1 us (12%)
  local copies, waits for them, and re-layouts  29.2 us (10%)
  other arithmetic  26.6 us (9%)
  matrix products  9.13 us (3%)
    ppermute x21, starting transfers between devices, turn(): lax.ppermute(array, AXES, [(i, i // 4 * 4 + (i + step) % 4) for i in rang...  43 us
    ppermute x21, waiting for transfers between devices, turn(): lax.ppermute(array, AXES, [(i, i // 4 * 4 + (i + step) % 4) for i in rang...  30.5 us
    ppermute x21, starting transfers between devices, swap_chips(): lax.ppermute(array, AXES, [(i, i ^ masks[i // 4 % 2]) for i in range(32)])  22.4 us
    unnamed x149, local copies, waits for them, and re-layouts  20.4 us
    pallas_call x3, Pallas kernels, wide_grad(): pl.pallas_call(functools.partial(wide_kernel, steps), grid_spec=pltpu.Pre...  19.7 us
    pallas_call x2, Pallas kernels, attend_back(): pl.pallas_call(functools.partial(attend_back_kernel, group * width // HDI...  18.4 us
    pallas_call x1, Pallas kernels, ease_two(): pl.pallas_call(ease_two_kernel, grid=(count // some,), in_specs=[rows(hid...  12.4 us
    pallas_call x1, Pallas kernels, attend(): pl.pallas_call(attend_kernel, grid=(frames,), in_specs=[pl.BlockSpec((PAD...  11 us
  transfers between devices with their start and end apart: 59, of which 13 were waited for; matrix products, arithmetic and copies ran while one was open for 12% of the time, Pallas kernels for 31%

profile of v1, /device:TPU:0, one launch (start us, length us, event | category | flops | bytes accessed | tf_op | source)
XLA Modules:
  0.0 298.4 jit_solution(16182005463232498240)
XLA Ops:
  3.1 4.0 %collective-permute-start.1 = (bf16[24,3328]{1,0:T(8,128)(2,1)}, bf16[24,3328]{1,0:T(8,128)(2,1)S(1)}, u32[]{:S(2)}, u32[]{:S(2)}) collective-permute-start(bf16[24,3328]{1,0:T(8,128)(2,1)} %pack.1), channel_id=1, source_target_pairs={{0,2},{1,3},{2,0},{3,1},{4,6},{5,7},{6,4},{7,5},{8,10},{9,11},{10,... | collective-permute-start | bytes 479240 | tf_op jit(solution)/shard_map/ppermute | solution.py:478
  9.1 7.4 %collective-permute-done.1 = bf16[24,3328]{1,0:T(8,128)(2,1)S(1)} collective-permute-done((bf16[24,3328]{1,0:T(8,128)(2,1)}, bf16[24,3328]{1,0:T(8,128)(2,1)S(1)}, u32[]{:S(2)}, u32[]{:S(2)}) %collective-permute-start.1) | collective-permute-done | bytes 159776 | tf_op jit(solution)/shard_map/ppermute | solution.py:478
  16.5 3.0 %collective-permute-done = bf16[24,3328]{1,0:T(8,128)(2,1)S(1)} collective-permute-done((bf16[24,3328]{1,0:T(8,128)(2,1)}, bf16[24,3328]{1,0:T(8,128)(2,1)S(1)}, u32[]{:S(2)}, u32[]{:S(2)}) %collective-permute-start) | collective-permute-done | bytes 159776 | tf_op jit(solution)/shard_map/ppermute | solution.py:478
  22.1 3.1 %collective-permute-start.4 = (bf16[24,3072]{1,0:T(8,128)(2,1)S(1)}, bf16[24,3072]{1,0:T(8,128)(2,1)S(1)}, u32[]{:S(2)}, u32[]{:S(2)}) collective-permute-start(bf16[24,3072]{1,0:T(8,128)(2,1)S(1)} %copy-done.56), channel_id=1, source_target_pairs={{0,1},{1,2},{2,3},{3,0},{4,5},{5,6},{6,7},{7,4},{8,9},{9,10},{10,1... | collective-permute-start | bytes 442376 | tf_op jit(solution)/shard_map/ppermute | solution.py:478
  25.2 1.8 collective-permute-start.5
  27.0 2.9 collective-permute-start.6
  31.4 4.6 %collective-permute-done.5 = bf16[24,3072]{1,0:T(8,128)(2,1)S(1)} collective-permute-done((bf16[24,3072]{1,0:T(8,128)(2,1)S(1)}, bf16[24,3072]{1,0:T(8,128)(2,1)S(1)}, u32[]{:S(2)}, u32[]{:S(2)}) %collective-permute-start.5) | collective-permute-done | bytes 147488 | tf_op jit(solution)/shard_map/ppermute | solution.py:478
  39.0 2.3 reshape.238
  42.9 4.0 %collective-permute-start.10 = (bf16[96,768]{1,0:T(8,128)(2,1)S(1)}, bf16[96,768]{1,0:T(8,128)(2,1)S(1)}, u32[]{:S(2)}, u32[]{:S(2)}) collective-permute-start(bf16[96,768]{1,0:T(8,128)(2,1)S(1)} %copy-done.57), channel_id=1, source_target_pairs={{0,1},{1,2},{2,3},{3,0},{4,5},{5,6},{6,7},{7,4},{8,9},{9,10},{10,1... | collective-permute-start | bytes 442376 | tf_op jit(solution)/shard_map/ppermute | solution.py:478
  47.0 3.4 %collective-permute-start.11 = (bf16[96,768]{1,0:T(8,128)(2,1)S(1)}, bf16[96,768]{1,0:T(8,128)(2,1)S(1)}, u32[]{:S(2)}, u32[]{:S(2)}) collective-permute-start(bf16[96,768]{1,0:T(8,128)(2,1)S(1)} %copy-done.57), channel_id=1, source_target_pairs={{0,2},{1,3},{2,0},{3,1},{4,6},{5,7},{6,4},{7,5},{8,10},{9,11},{10,... | collective-permute-start | bytes 442376 | tf_op jit(solution)/shard_map/ppermute | solution.py:478
  50.4 2.5 collective-permute-start.12
  54.7 4.6 %collective-permute-done.11 = bf16[96,768]{1,0:T(8,128)(2,1)S(1)} collective-permute-done((bf16[96,768]{1,0:T(8,128)(2,1)S(1)}, bf16[96,768]{1,0:T(8,128)(2,1)S(1)}, u32[]{:S(2)}, u32[]{:S(2)}) %collective-permute-start.11) | collective-permute-done | bytes 147488 | tf_op jit(solution)/shard_map/ppermute | solution.py:478
  66.1 2.2 lay.3
  72.5 2.5 unfold.1
  79.9 1.9 fusion.2.refs_0_.qkv_ref
  81.8 1.8 fusion.3.refs_1_.qkv_ref
  83.7 11.0 %attend.1 = (bf16[832,768]{1,0:T(8,128)(2,1)S(1)}, f32[4,16,208]{2,1,0:T(8,128)S(1)}) custom-call(bf16[832,1152]{1,0:T(8,128)(2,1)S(1)} %fusion.2.refs_0_.qkv_ref, bf16[832,1152]{1,0:T(8,128)(2,1)S(1)} %fusion.3.refs_1_.qkv_ref), custom_call_target="tpu_custom_call" | custom-call | flops 44000002048 | tf_op jit(solution)/shard_map/attend/pallas_call | solution.py:114
  101.3 2.4 lay.4
  103.8 9.7 %widen.1 = (bf16[832,3072]{1,0:T(8,128)(2,1)S(1)}, bf16[832,3072]{1,0:T(8,128)(2,1)S(1)}) custom-call(bf16[832,768]{1,0:T(8,128)(2,1)S(1)} %add_convert_fusion.rows_ref.refs_0_, bf16[768,3072]{1,0:T(8,128)(2,1)S(1)} %bitcast.118, f32[1,3072]{1,0:T(1,128)S(1)} %copy-done.36), custom_call_target="tpu_custom_call" | custom-call | flops 38799998976 | tf_op jit(solution)/shard_map/widen/pallas_call | solution.py:200
  113.5 2.3 copy-done.28
  115.8 2.3 copy-done.29
  120.4 2.0 fusion.14.refs_0_
  122.4 2.9 lay.5
  125.4 4.2 %add_add_fusion.second_ref = f32[832,768]{1,0:T(8,128)S(1)} fusion(f32[832,768]{1,0:T(8,128)S(1)} %get-tuple-element.332.first_ref, bf16[832,3072]{1,0:T(8,128)(2,1)S(1)} %bitcast.132, bf16[3072,768]{1,0:T(8,128)(2,1)S(1)} %bitcast.120, f32[768]{0:T(1024)S(1)} %reduce.9), kind=kOutput, calls=%fused_computation.21 | convolution fusion | flops 3927146496 | bytes 14945280 | tf_op jit(solution)/shard_map/dot_general | solution.py:33
  129.6 9.6 %learn.1 = (f32[32,768]{1,0:T(8,128)S(1)}, f32[832,768]{1,0:T(8,128)S(1)}, bf16[832,768]{1,0:T(8,128)(2,1)S(1)}, f32[8,768]{1,0:T(8,128)S(1)}, f32[768,128]{1,0:...) custom-call(s32[1]{0:T(128)S(6)} %copy.51.refs_10_.live_ref, f32[1,128]{1,0:T(1,128)S(1)} %copy-done.48, ...), custom_call_target="tpu_custom_call" | custom-call | flops 40800002048 | tf_op jit(solution)/shard_map/learn/pallas_call | solution.py:322
  142.1 8.4 %tall_grad.1 = (bf16[4,384,768]{2,1,0:T(8,128)(2,1)S(1)}, bf16[4,384,768]{2,1,0:T(8,128)(2,1)S(1)}) custom-call(s32[8]{0:T(128)S(1)} %stack.53.order_ref, bf16[832,3072]{1,0:T(8,128)(2,1)S(1)} %bitcast.132, bf16[832,768]{1,0:T(8,128)(2,1)S(1)} %get-tuple-element.178.right_ref.grad_ref), custom_call_target="tpu_custom_call" | custom-call | flops 33600000000 | tf_op jit(solution)/shard_map/tall_grad/pallas_call | solution.py:592
  150.7 8.4 %steep.1 = (bf16[832,3072]{1,0:T(8,128)(2,1)S(1)}, f32[1,3072]{1,0:T(1,128)S(1)}) custom-call(bf16[832,768]{1,0:T(8,128)(2,1)S(1)} %get-tuple-element.178.right_ref.grad_ref, bf16[3072,768]{1,0:T(8,128)(2,1)S(1)} %bitcast.121, bf16[832,3072]{1,0:T(8,128)(2,1)S(1)} %bitcast.134), custom_call_target="tpu_custom_call" | custom-call | flops 33600000000 | tf_op jit(solution)/shard_map/steep/pallas_call | solution.py:226
  161.3 7.6 %wide_grad.3 = (bf16[4,96,3072]{2,1,0:T(8,128)(2,1)S(1)}, bf16[4,96,3072]{2,1,0:T(8,128)(2,1)S(1)}) custom-call(s32[8]{0:T(128)S(1)} %stack.53.order_ref, bf16[832,768]{1,0:T(8,128)(2,1)S(1)} %copy-done.4, bf16[832,3072]{1,0:T(8,128)(2,1)S(1)} %get-tuple-element.186.refs_1_.grad_ref), custom_call_target="tpu_custom_call" | custom-call | flops 33491200000 | tf_op jit(solution)/shard_map/wide_grad/pallas_call | solution.py:649
  168.9 2.3 copy-done.30
  174.5 12.4 %ease_two.1 = (f32[832,768]{1,0:T(8,128)S(1)}, bf16[832,768]{1,0:T(8,128)(2,1)S(1)}, bf16[832,768]{1,0:T(8,128)(2,1)S(1)}, f32[8,768]{1,0:T(8,128)S(1)}) custom-call(bf16[832,3072]{1,0:T(8,128)(2,1)} %copy-done.30, bf16[768,3072]{1,0:T(8,128)(2,1)} %bitcast.119, f32[832,768]{1,0:T(8,128)S(1)} %get-tuple-element.332.first_ref, f32[1,768]{1,0:T(1,128)S(1)} %copy-done.7, ...), custom_call_target="tpu_custom_call" | custom-call | flops 48000000000 | tf_op jit(solution)/shard_map/ease_two/pallas_call | solution.py:398
  191.2 3.4 %collective-permute-start.36 = (bf16[96,768]{1,0:T(8,128)(2,1)S(1)}, bf16[96,768]{1,0:T(8,128)(2,1)S(1)}, u32[]{:S(2)}, u32[]{:S(2)}) collective-permute-start(bf16[96,768]{1,0:T(8,128)(2,1)S(1)} %get-tuple-element.308), channel_id=1, source_target_pairs={{0,1},{1,2},{2,3},{3,0},{4,5},{5,6},{6,7},{7,4},{8,9},{9,10},{10,1... | collective-permute-start | bytes 442376 | tf_op jit(solution)/shard_map/ppermute | solution.py:478
  198.4 9.2 %attend_back.2 = (bf16[832,1152]{1,0:T(8,128)(2,1)S(1)}, f32[8,1152]{1,0:T(8,128)S(1)}) custom-call(bf16[832,1152]{1,0:T(8,128)(2,1)S(1)} %copy-done.27, f32[4,16,208]{2,1,0:T(8,128)S(1)} %copy-done.43, bf16[832,768]{1,0:T(8,128)(2,1)S(1)} %get-tuple-element.200.grad_ref), custom_call_target="tpu_custom_call" | custom-call | flops 36800000000 | tf_op jit(solution)/shard_map/attend_back/pallas_call | solution.py:168
  207.6 7.2 %wide_grad.4 = (bf16[4,96,1920]{2,1,0:T(8,128)(2,1)S(1)}, bf16[4,96,1920]{2,1,0:T(8,128)(2,1)S(1)}) custom-call(s32[8]{0:T(128)S(1)} %stack.53.order_ref, bf16[832,768]{1,0:T(8,128)(2,1)S(1)} %fusion.14.refs_0_, bf16[832,768]{1,0:T(8,128)(2,1)S(1)} %copy-done.23, bf16[832,1152]{1,0:T(8,128)(2,1)S(1)} %get-tuple-element.208.refs_2_.refs_0_, ...), custom_call_target="tpu_custom_call" | custom-call | flops 22432000000 | tf_op jit(solution)/shard_map/wide_grad/pallas_call | solution.py:649
  216.9 9.2 %attend_back.3 = (bf16[832,1152]{1,0:T(8,128)(2,1)S(1)}, f32[8,1152]{1,0:T(8,128)S(1)}) custom-call(bf16[832,1152]{1,0:T(8,128)(2,1)S(1)} %copy-done.25, f32[4,16,208]{2,1,0:T(8,128)S(1)} %copy-done.43, bf16[832,768]{1,0:T(8,128)(2,1)S(1)} %get-tuple-element.200.grad_ref), custom_call_target="tpu_custom_call" | custom-call | flops 36800000000 | tf_op jit(solution)/shard_map/attend_back/pallas_call | solution.py:168
  226.9 5.0 %wide_grad.5 = (bf16[4,96,1152]{2,1,0:T(8,128)(2,1)}, bf16[4,96,1152]{2,1,0:T(8,128)(2,1)S(1)}) custom-call(s32[8]{0:T(128)S(1)} %stack.53.order_ref, bf16[832,768]{1,0:T(8,128)(2,1)S(1)} %fusion.14.refs_0_, bf16[832,1152]{1,0:T(8,128)(2,1)S(1)} %get-tuple-element.204.refs_1_), custom_call_target="tpu_custom_call" | custom-call | flops 15059200000 | tf_op jit(solution)/shard_map/wide_grad/pallas_call | solution.py:649
  234.8 2.0 collective-permute-start.44
  241.2 6.2 %ease_one.1 = (f32[4,196,768]{2,1,0:T(8,128)S(1)}, f32[8,768]{1,0:T(8,128)S(1)}) custom-call(bf16[832,1152]{1,0:T(8,128)(2,1)S(1)} %get-tuple-element.208.refs_2_.refs_0_, bf16[832,1152]{1,0:T(8,128)(2,1)S(1)} %get-tuple-element.204.refs_1_, bf16[768,1152]{1,0:T(8,128)(2,1)S(1)} %bitcast.123, bf16[768,1152]{1,0:T(8,128)(2,1)S(1)} %bitcast.125, ...), custom_call_target="tpu_custom_call" | custom-call | flops 25200001024 | tf_op jit(solution)/shard_map/ease_one/pallas_call | solution.py:443
  247.5 1.9 fusion.19
  252.6 4.8 %payload.1 = f32[32,24,128]{2,1,0:T(8,128)} custom-call(f32[8,768]{1,0:T(8,128)} %copy-done.39, f32[8,768]{1,0:T(8,128)} %copy-done.40, f32[8,768]{1,0:T(8,128)} %copy-done.41, f32[1,3072]{1,0:T(1,128)} %copy-done.44, f32[8,1152]{1,0:T(8,128)} %copy-done.37, f32[8,1152]{1,0:T(8,128)} %copy-done.38, f32[32,24,128]{2,1,0:T(8,128)} %bitcast.128, ...), custom_call_target="tpu_custom_call" | custom-call | flops 18800001024 | tf_op jit(solution)/shard_map/payload/pallas_call | solution.py:984
  257.4 3.3 %all-to-all-start = ((f32[32,24,128]{2,1,0:T(8,128)}), f32[32,24,128]{2,1,0:T(8,128)S(1)}, u32[]{:S(2)}, u32[]{:S(2)}) async-start(f32[32,24,128]{2,1,0:T(8,128)} %payload.1), calls=%async_computation | async-start | bytes 786432 | tf_op jit(solution)/shard_map/all_to_all | solution.py:706
  261.9 1.8 collective-permute-start.47
  264.0 1.9 bitcast_add_fusion.9
  265.9 3.8 %collective-permute-done.47 = bf16[96,1152]{1,0:T(8,128)(2,1)S(1)} collective-permute-done((bf16[96,1152]{1,0:T(8,128)(2,1)S(1)}, bf16[96,1152]{1,0:T(8,128)(2,1)S(1)}, u32[]{:S(2)}, u32[]{:S(2)}) %collective-permute-start.47) | collective-permute-done | bytes 221216 | tf_op jit(solution)/shard_map/ppermute | solution.py:474
  271.2 3.8 %collective-permute-start.52 = (bf16[24,1920]{1,0:T(8,128)(2,1)S(1)}, bf16[24,1920]{1,0:T(8,128)(2,1)S(1)}, u32[]{:S(2)}, u32[]{:S(2)}) collective-permute-start(bf16[24,1920]{1,0:T(8,128)(2,1)S(1)} %get-tuple-element.310), channel_id=1, source_target_pairs={{0,3},{1,0},{2,1},{3,2},{4,7},{5,4},{6,5},{7,6},{8,11},{9,8},{10,9... | collective-permute-start | bytes 276488 | tf_op jit(solution)/shard_map/ppermute | solution.py:478
  278.7 4.5 %collective-permute-done.51 = bf16[24,1920]{1,0:T(8,128)(2,1)S(1)} collective-permute-done((bf16[24,1920]{1,0:T(8,128)(2,1)S(1)}, bf16[24,1920]{1,0:T(8,128)(2,1)S(1)}, u32[]{:S(2)}, u32[]{:S(2)}) %collective-permute-start.51) | collective-permute-done | bytes 92192 | tf_op jit(solution)/shard_map/ppermute | solution.py:478
  284.3 2.7 collective-permute-start.57
  289.3 2.7 collective-permute-done.56
  292.0 2.0 collective-permute-done.55
  (303 shorter events, 82.8 us)
Async XLA Ops:
  3.1 13.4 %collective-permute-start.1 = (bf16[24,3328]{1,0:T(8,128)(2,1)}, bf16[24,3328]{1,0:T(8,128)(2,1)S(1)}, u32[]{:S(2)}, u32[]{:S(2)}) collective-permute-start(bf16[24,3328]{1,0:T(8,128)(2,1)} %pack.1), channel_id=1, source_target_pairs={{0,2},{1,3},{2,0},{3,1},{4,6},{5,7},{6,4},{7,5},{8,10},{9,11},{10,... | collective-permute-start | bytes 479240 | tf_op jit(solution)/shard_map/ppermute | solution.py:478
  7.1 9.4 %collective-permute-start.2 = (bf16[24,3328]{1,0:T(8,128)(2,1)}, bf16[24,3328]{1,0:T(8,128)(2,1)S(1)}, u32[]{:S(2)}, u32[]{:S(2)}) collective-permute-start(bf16[24,3328]{1,0:T(8,128)(2,1)} %pack.1), channel_id=1, source_target_pairs={{0,3},{1,0},{2,1},{3,2},{4,7},{5,4},{6,5},{7,6},{8,11},{9,8},{10,9... | collective-permute-start | bytes 479240 | tf_op jit(solution)/shard_map/ppermute | solution.py:478
  8.5 11.0 %collective-permute-start = (bf16[24,3328]{1,0:T(8,128)(2,1)}, bf16[24,3328]{1,0:T(8,128)(2,1)S(1)}, u32[]{:S(2)}, u32[]{:S(2)}) collective-permute-start(bf16[24,3328]{1,0:T(8,128)(2,1)} %pack.1), channel_id=1, source_target_pairs={{0,1},{1,2},{2,3},{3,0},{4,5},{5,6},{6,7},{7,4},{8,9},{9,10},{10,1... | collective-permute-start | bytes 479240 | tf_op jit(solution)/shard_map/ppermute | solution.py:478
  20.5 15.5 %collective-permute-start.3 = (bf16[96,3328]{1,0:T(8,128)(2,1)S(1)}, bf16[96,3328]{1,0:T(8,128)(2,1)S(1)}, u32[]{:S(2)}, u32[]{:S(2)}) collective-permute-start(bf16[96,3328]{1,0:T(8,128)(2,1)S(1)} %pad_maximum_fusion.refs_0_), channel_id=1, source_target_pairs={{0,8},{1,9},{2,10},{3,11},{4,20},{5,21},{6,22},{7,23},{8,0},{9,1},... | collective-permute-start | bytes 1916936 | tf_op jit(solution)/shard_map/ppermute | solution.py:474
  22.1 9.3 %collective-permute-start.4 = (bf16[24,3072]{1,0:T(8,128)(2,1)S(1)}, bf16[24,3072]{1,0:T(8,128)(2,1)S(1)}, u32[]{:S(2)}, u32[]{:S(2)}) collective-permute-start(bf16[24,3072]{1,0:T(8,128)(2,1)S(1)} %copy-done.56), channel_id=1, source_target_pairs={{0,1},{1,2},{2,3},{3,0},{4,5},{5,6},{6,7},{7,4},{8,9},{9,10},{10,1... | collective-permute-start | bytes 442376 | tf_op jit(solution)/shard_map/ppermute | solution.py:478
  25.2 10.8 %collective-permute-start.5 = (bf16[24,3072]{1,0:T(8,128)(2,1)S(1)}, bf16[24,3072]{1,0:T(8,128)(2,1)S(1)}, u32[]{:S(2)}, u32[]{:S(2)}) collective-permute-start(bf16[24,3072]{1,0:T(8,128)(2,1)S(1)} %copy-done.56), channel_id=1, source_target_pairs={{0,2},{1,3},{2,0},{3,1},{4,6},{5,7},{6,4},{7,5},{8,10},{9,11},{10,... | collective-permute-start | bytes 442376 | tf_op jit(solution)/shard_map/ppermute | solution.py:478
  27.0 9.0 %collective-permute-start.6 = (bf16[24,3072]{1,0:T(8,128)(2,1)S(1)}, bf16[24,3072]{1,0:T(8,128)(2,1)S(1)}, u32[]{:S(2)}, u32[]{:S(2)}) collective-permute-start(bf16[24,3072]{1,0:T(8,128)(2,1)S(1)} %copy-done.56), channel_id=1, source_target_pairs={{0,3},{1,0},{2,1},{3,2},{4,7},{5,4},{6,5},{7,6},{8,11},{9,8},{10,9... | collective-permute-start | bytes 442376 | tf_op jit(solution)/shard_map/ppermute | solution.py:478
  29.9 20.4 %collective-permute-start.8 = (bf16[96,3328]{1,0:T(8,128)(2,1)S(1)}, bf16[96,3328]{1,0:T(8,128)(2,1)S(1)}, u32[]{:S(2)}, u32[]{:S(2)}) collective-permute-start(bf16[96,3328]{1,0:T(8,128)(2,1)S(1)} %pad_maximum_fusion.refs_0_), channel_id=1, source_target_pairs={{0,16},{1,17},{2,18},{3,19},{4,12},{5,13},{6,14},{7,15},{8,24},{9,... | collective-permute-start | bytes 1916936 | tf_op jit(solution)/shard_map/ppermute | solution.py:474
  36.0 23.3 %collective-permute-start.7 = (bf16[96,3328]{1,0:T(8,128)(2,1)S(1)}, bf16[96,3328]{1,0:T(8,128)(2,1)S(1)}, u32[]{:S(2)}, u32[]{:S(2)}) collective-permute-start(bf16[96,3328]{1,0:T(8,128)(2,1)S(1)} %collective-permute-done.3.refs_1_), channel_id=1, source_target_pairs={{0,16},{1,17},{2,18},{3,19},{4,12},{5,13},{6,14},{7,15},{8,24},{9,... | collective-permute-start | bytes 1916936 | tf_op jit(solution)/shard_map/ppermute | solution.py:474
  38.0 21.3 %collective-permute-start.9 = (bf16[96,3072]{1,0:T(8,128)(2,1)}, bf16[96,3072]{1,0:T(8,128)(2,1)S(1)}, u32[]{:S(2)}, u32[]{:S(2)}) collective-permute-start(bf16[96,3072]{1,0:T(8,128)(2,1)} %pad_maximum_fusion.1.refs_0_), channel_id=1, source_target_pairs={{0,8},{1,9},{2,10},{3,11},{4,20},{5,21},{6,22},{7,23},{8,0},{9,1},... | collective-permute-start | bytes 1769480 | tf_op jit(solution)/shard_map/ppermute | solution.py:474
  42.9 11.8 %collective-permute-start.10 = (bf16[96,768]{1,0:T(8,128)(2,1)S(1)}, bf16[96,768]{1,0:T(8,128)(2,1)S(1)}, u32[]{:S(2)}, u32[]{:S(2)}) collective-permute-start(bf16[96,768]{1,0:T(8,128)(2,1)S(1)} %copy-done.57), channel_id=1, source_target_pairs={{0,1},{1,2},{2,3},{3,0},{4,5},{5,6},{6,7},{7,4},{8,9},{9,10},{10,1... | collective-permute-start | bytes 442376 | tf_op jit(solution)/shard_map/ppermute | solution.py:478
  47.0 12.3 %collective-permute-start.11 = (bf16[96,768]{1,0:T(8,128)(2,1)S(1)}, bf16[96,768]{1,0:T(8,128)(2,1)S(1)}, u32[]{:S(2)}, u32[]{:S(2)}) collective-permute-start(bf16[96,768]{1,0:T(8,128)(2,1)S(1)} %copy-done.57), channel_id=1, source_target_pairs={{0,2},{1,3},{2,0},{3,1},{4,6},{5,7},{6,4},{7,5},{8,10},{9,11},{10,... | collective-permute-start | bytes 442376 | tf_op jit(solution)/shard_map/ppermute | solution.py:478
  50.4 8.9 %collective-permute-start.12 = (bf16[96,768]{1,0:T(8,128)(2,1)S(1)}, bf16[96,768]{1,0:T(8,128)(2,1)S(1)}, u32[]{:S(2)}, u32[]{:S(2)}) collective-permute-start(bf16[96,768]{1,0:T(8,128)(2,1)S(1)} %copy-done.57), channel_id=1, source_target_pairs={{0,3},{1,0},{2,1},{3,2},{4,7},{5,4},{6,5},{7,6},{8,11},{9,8},{10,9... | collective-permute-start | bytes 442376 | tf_op jit(solution)/shard_map/ppermute | solution.py:478
  54.7 9.1 %collective-permute-start.13 = (bf16[96,3328]{1,0:T(8,128)(2,1)S(1)}, bf16[96,3328]{1,0:T(8,128)(2,1)S(1)}, u32[]{:S(2)}, u32[]{:S(2)}) collective-permute-start(bf16[96,3328]{1,0:T(8,128)(2,1)S(1)} %pad_maximum_fusion.refs_0_), channel_id=1, source_target_pairs={{0,4},{1,5},{2,6},{3,7},{4,0},{5,1},{6,2},{7,3},{8,12},{9,13},{10,... | collective-permute-start | bytes 1916936 | tf_op jit(solution)/shard_map/ppermute | solution.py:469
  61.9 35.4 %collective-permute-start.17 = (bf16[96,3072]{1,0:T(8,128)(2,1)}, bf16[96,3072]{1,0:T(8,128)(2,1)}, u32[]{:S(2)}, u32[]{:S(2)}) collective-permute-start(bf16[96,3072]{1,0:T(8,128)(2,1)} %pad_maximum_fusion.1.refs_0_), channel_id=1, source_target_pairs={{0,16},{1,17},{2,18},{3,19},{4,12},{5,13},{6,14},{7,15},{8,24},{9,... | collective-permute-start | bytes 1769480 | tf_op jit(solution)/shard_map/ppermute | solution.py:474
  63.8 34.4 %collective-permute-start.20 = (bf16[96,3072]{1,0:T(8,128)(2,1)}, bf16[96,3072]{1,0:T(8,128)(2,1)}, u32[]{:S(2)}, u32[]{:S(2)}) collective-permute-start(bf16[96,3072]{1,0:T(8,128)(2,1)} %pad_maximum_fusion.1.refs_0_), channel_id=1, source_target_pairs={{0,4},{1,5},{2,6},{3,7},{4,0},{5,1},{6,2},{7,3},{8,12},{9,13},{10,... | collective-permute-start | bytes 1769480 | tf_op jit(solution)/shard_map/ppermute | solution.py:469
  63.9 33.4 %collective-permute-start.18 = (bf16[96,3072]{1,0:T(8,128)(2,1)}, bf16[96,3072]{1,0:T(8,128)(2,1)}, u32[]{:S(2)}, u32[]{:S(2)}) collective-permute-start(bf16[96,3072]{1,0:T(8,128)(2,1)} %copy-done.8), channel_id=1, source_target_pairs={{0,16},{1,17},{2,18},{3,19},{4,12},{5,13},{6,14},{7,15},{8,24},{9,... | collective-permute-start | bytes 1769480 | tf_op jit(solution)/shard_map/ppermute | solution.py:474
  64.3 33.9 %collective-permute-start.21 = (bf16[96,3072]{1,0:T(8,128)(2,1)}, bf16[96,3072]{1,0:T(8,128)(2,1)}, u32[]{:S(2)}, u32[]{:S(2)}) collective-permute-start(bf16[96,3072]{1,0:T(8,128)(2,1)} %copy-done.8), channel_id=1, source_target_pairs={{0,4},{1,5},{2,6},{3,7},{4,0},{5,1},{6,2},{7,3},{8,12},{9,13},{10,... | collective-permute-start | bytes 1769480 | tf_op jit(solution)/shard_map/ppermute | solution.py:469
  64.5 32.9 %collective-permute-start.19 = (bf16[384,768]{1,0:T(8,128)(2,1)S(1)}, bf16[384,768]{1,0:T(8,128)(2,1)}, u32[]{:S(2)}, u32[]{:S(2)}) collective-permute-start(bf16[384,768]{1,0:T(8,128)(2,1)S(1)} %pad_maximum_fusion.2.refs_0_), channel_id=1, source_target_pairs={{0,8},{1,9},{2,10},{3,11},{4,20},{5,21},{6,22},{7,23},{8,0},{9,1},... | collective-permute-start | bytes 1769480 | tf_op jit(solution)/shard_map/ppermute | solution.py:474
  97.9 20.2 %collective-permute-start.24 = (bf16[384,768]{1,0:T(8,128)(2,1)S(1)}, bf16[384,768]{1,0:T(8,128)(2,1)}, u32[]{:S(2)}, u32[]{:S(2)}) collective-permute-start(bf16[384,768]{1,0:T(8,128)(2,1)S(1)} %pad_maximum_fusion.2.refs_0_), channel_id=1, source_target_pairs={{0,16},{1,17},{2,18},{3,19},{4,12},{5,13},{6,14},{7,15},{8,24},{9,... | collective-permute-start | bytes 1769480 | tf_op jit(solution)/shard_map/ppermute | solution.py:474
  98.2 24.2 %collective-permute-start.26 = (bf16[384,768]{1,0:T(8,128)(2,1)S(1)}, bf16[384,768]{1,0:T(8,128)(2,1)}, u32[]{:S(2)}, u32[]{:S(2)}) collective-permute-start(bf16[384,768]{1,0:T(8,128)(2,1)S(1)} %pad_maximum_fusion.2.refs_0_), channel_id=1, source_target_pairs={{0,4},{1,5},{2,6},{3,7},{4,0},{5,1},{6,2},{7,3},{8,12},{9,13},{10,... | collective-permute-start | bytes 1769480 | tf_op jit(solution)/shard_map/ppermute | solution.py:469
  98.2 19.9 %collective-permute-start.25 = (bf16[384,768]{1,0:T(8,128)(2,1)}, bf16[384,768]{1,0:T(8,128)(2,1)}, u32[]{:S(2)}, u32[]{:S(2)}) collective-permute-start(bf16[384,768]{1,0:T(8,128)(2,1)} %collective-permute-done.19.refs_1_), channel_id=1, source_target_pairs={{0,16},{1,17},{2,18},{3,19},{4,12},{5,13},{6,14},{7,15},{8,24},{9,... | collective-permute-start | bytes 1769480 | tf_op jit(solution)/shard_map/ppermute | solution.py:474
  100.0 22.4 %collective-permute-start.27 = (bf16[384,768]{1,0:T(8,128)(2,1)}, bf16[384,768]{1,0:T(8,128)(2,1)}, u32[]{:S(2)}, u32[]{:S(2)}) collective-permute-start(bf16[384,768]{1,0:T(8,128)(2,1)} %collective-permute-done.19.refs_1_), channel_id=1, source_target_pairs={{0,4},{1,5},{2,6},{3,7},{4,0},{5,1},{6,2},{7,3},{8,12},{9,13},{10,... | collective-permute-start | bytes 1769480 | tf_op jit(solution)/shard_map/ppermute | solution.py:469
  150.5 8.6 %collective-permute-start.30 = (bf16[4,384,768]{2,1,0:T(8,128)(2,1)S(1)}, bf16[4,384,768]{2,1,0:T(8,128)(2,1)S(1)}, u32[]{:S(2)}, u32[]{:S(2)}) collective-permute-start(bf16[4,384,768]{2,1,0:T(8,128)(2,1)S(1)} %get-tuple-element.181), channel_id=1, source_target_pairs={{0,4},{1,5},{2,6},{3,7},{4,0},{5,1},{6,2},{7,3},{8,12},{9,13},{10,... | collective-permute-start | bytes 7077896 | tf_op jit(solution)/shard_map/ppermute | solution.py:469
  159.7 12.0 %collective-permute-start.31 = (bf16[384,768]{1,0:T(8,128)(2,1)S(1)}, bf16[384,768]{1,0:T(8,128)(2,1)S(1)}, u32[]{:S(2)}, u32[]{:S(2)}) collective-permute-start(bf16[384,768]{1,0:T(8,128)(2,1)S(1)} %get-tuple-element.298), channel_id=1, source_target_pairs={{0,16},{1,17},{2,18},{3,19},{4,12},{5,13},{6,14},{7,15},{8,24},{9,... | collective-permute-start | bytes 1769480 | tf_op jit(solution)/shard_map/ppermute | solution.py:474
  171.3 16.0 %collective-permute-start.32 = (bf16[4,96,3072]{2,1,0:T(8,128)(2,1)S(1)}, bf16[4,96,3072]{2,1,0:T(8,128)(2,1)S(1)}, u32[]{:S(2)}, u32[]{:S(2)}) collective-permute-start(bf16[4,96,3072]{2,1,0:T(8,128)(2,1)S(1)} %get-tuple-element.189), channel_id=1, source_target_pairs={{0,4},{1,5},{2,6},{3,7},{4,0},{5,1},{6,2},{7,3},{8,12},{9,13},{10,... | collective-permute-start | bytes 7077896 | tf_op jit(solution)/shard_map/ppermute | solution.py:469
  171.6 15.6 %collective-permute-start.34 = (bf16[384,768]{1,0:T(8,128)(2,1)S(1)}, bf16[384,768]{1,0:T(8,128)(2,1)S(1)}, u32[]{:S(2)}, u32[]{:S(2)}) collective-permute-start(bf16[384,768]{1,0:T(8,128)(2,1)S(1)} %get-tuple-element.297), channel_id=1, source_target_pairs={{0,16},{1,17},{2,18},{3,19},{4,12},{5,13},{6,14},{7,15},{8,24},{9,... | collective-permute-start | bytes 1769480 | tf_op jit(solution)/shard_map/ppermute | solution.py:474
  172.8 14.5 %collective-permute-start.33 = (bf16[384,768]{1,0:T(8,128)(2,1)}, bf16[384,768]{1,0:T(8,128)(2,1)S(1)}, u32[]{:S(2)}, u32[]{:S(2)}) collective-permute-start(bf16[384,768]{1,0:T(8,128)(2,1)} %fusion.18), channel_id=1, source_target_pairs={{0,8},{1,9},{2,10},{3,11},{4,20},{5,21},{6,22},{7,23},{8,0},{9,1},... | collective-permute-start | bytes 1769480 | tf_op jit(solution)/shard_map/ppermute | solution.py:474
  189.2 18.4 %collective-permute-start.35 = (bf16[96,3072]{1,0:T(8,128)(2,1)S(1)}, bf16[96,3072]{1,0:T(8,128)(2,1)S(1)}, u32[]{:S(2)}, u32[]{:S(2)}) collective-permute-start(bf16[96,3072]{1,0:T(8,128)(2,1)S(1)} %get-tuple-element.296), channel_id=1, source_target_pairs={{0,16},{1,17},{2,18},{3,19},{4,12},{5,13},{6,14},{7,15},{8,24},{9,... | collective-permute-start | bytes 1769480 | tf_op jit(solution)/shard_map/ppermute | solution.py:474
  191.2 16.4 %collective-permute-start.36 = (bf16[96,768]{1,0:T(8,128)(2,1)S(1)}, bf16[96,768]{1,0:T(8,128)(2,1)S(1)}, u32[]{:S(2)}, u32[]{:S(2)}) collective-permute-start(bf16[96,768]{1,0:T(8,128)(2,1)S(1)} %get-tuple-element.308), channel_id=1, source_target_pairs={{0,1},{1,2},{2,3},{3,0},{4,5},{5,6},{6,7},{7,4},{8,9},{9,10},{10,1... | collective-permute-start | bytes 442376 | tf_op jit(solution)/shard_map/ppermute | solution.py:478
  194.6 13.0 %collective-permute-start.37 = (bf16[96,768]{1,0:T(8,128)(2,1)S(1)}, bf16[96,768]{1,0:T(8,128)(2,1)S(1)}, u32[]{:S(2)}, u32[]{:S(2)}) collective-permute-start(bf16[96,768]{1,0:T(8,128)(2,1)S(1)} %get-tuple-element.307), channel_id=1, source_target_pairs={{0,2},{1,3},{2,0},{3,1},{4,6},{5,7},{6,4},{7,5},{8,10},{9,11},{10,... | collective-permute-start | bytes 442376 | tf_op jit(solution)/shard_map/ppermute | solution.py:478
  196.0 11.6 %collective-permute-start.38 = (bf16[96,768]{1,0:T(8,128)(2,1)S(1)}, bf16[96,768]{1,0:T(8,128)(2,1)S(1)}, u32[]{:S(2)}, u32[]{:S(2)}) collective-permute-start(bf16[96,768]{1,0:T(8,128)(2,1)S(1)} %get-tuple-element.306), channel_id=1, source_target_pairs={{0,3},{1,0},{2,1},{3,2},{4,7},{5,4},{6,5},{7,6},{8,11},{9,8},{10,9... | collective-permute-start | bytes 442376 | tf_op jit(solution)/shard_map/ppermute | solution.py:478
  197.0 29.9 %collective-permute-start.41 = (bf16[96,3072]{1,0:T(8,128)(2,1)S(1)}, bf16[96,3072]{1,0:T(8,128)(2,1)S(1)}, u32[]{:S(2)}, u32[]{:S(2)}) collective-permute-start(bf16[96,3072]{1,0:T(8,128)(2,1)S(1)} %get-tuple-element.295), channel_id=1, source_target_pairs={{0,16},{1,17},{2,18},{3,19},{4,12},{5,13},{6,14},{7,15},{8,24},{9,... | collective-permute-start | bytes 1769480 | tf_op jit(solution)/shard_map/ppermute | solution.py:474
  214.8 12.1 %collective-permute-start.39 = (bf16[4,96,1920]{2,1,0:T(8,128)(2,1)S(1)}, bf16[4,96,1920]{2,1,0:T(8,128)(2,1)S(1)}, u32[]{:S(2)}, u32[]{:S(2)}) collective-permute-start(bf16[4,96,1920]{2,1,0:T(8,128)(2,1)S(1)} %get-tuple-element.202), channel_id=1, source_target_pairs={{0,4},{1,5},{2,6},{3,7},{4,0},{5,1},{6,2},{7,3},{8,12},{9,13},{10,... | collective-permute-start | bytes 4423688 | tf_op jit(solution)/shard_map/ppermute | solution.py:469
  215.1 11.7 %collective-permute-start.40 = (bf16[96,3072]{1,0:T(8,128)(2,1)S(1)}, bf16[96,3072]{1,0:T(8,128)(2,1)S(1)}, u32[]{:S(2)}, u32[]{:S(2)}) collective-permute-start(bf16[96,3072]{1,0:T(8,128)(2,1)S(1)} %fusion.16), channel_id=1, source_target_pairs={{0,8},{1,9},{2,10},{3,11},{4,20},{5,21},{6,22},{7,23},{8,0},{9,1},... | collective-permute-start | bytes 1769480 | tf_op jit(solution)/shard_map/ppermute | solution.py:474
  232.8 7.5 %collective-permute-start.42 = (bf16[96,1920]{1,0:T(8,128)(2,1)S(1)}, bf16[96,1920]{1,0:T(8,128)(2,1)S(1)}, u32[]{:S(2)}, u32[]{:S(2)}) collective-permute-start(bf16[96,1920]{1,0:T(8,128)(2,1)S(1)} %get-tuple-element.300), channel_id=1, source_target_pairs={{0,16},{1,17},{2,18},{3,19},{4,12},{5,13},{6,14},{7,15},{8,24},{9,... | collective-permute-start | bytes 1105928 | tf_op jit(solution)/shard_map/ppermute | solution.py:474
  233.7 18.9 %collective-permute-start.43 = (bf16[4,96,1152]{2,1,0:T(8,128)(2,1)}, bf16[4,96,1152]{2,1,0:T(8,128)(2,1)}, u32[]{:S(2)}, u32[]{:S(2)}) collective-permute-start(bf16[4,96,1152]{2,1,0:T(8,128)(2,1)} %get-tuple-element.214), channel_id=1, source_target_pairs={{0,4},{1,5},{2,6},{3,7},{4,0},{5,1},{6,2},{7,3},{8,12},{9,13},{10,... | collective-permute-start | bytes 2654216 | tf_op jit(solution)/shard_map/ppermute | solution.py:469
  234.8 16.1 %collective-permute-start.44 = (bf16[24,3072]{1,0:T(8,128)(2,1)}, bf16[24,3072]{1,0:T(8,128)(2,1)S(1)}, u32[]{:S(2)}, u32[]{:S(2)}) collective-permute-start(bf16[24,3072]{1,0:T(8,128)(2,1)} %get-tuple-element.305), channel_id=1, source_target_pairs={{0,1},{1,2},{2,3},{3,0},{4,5},{5,6},{6,7},{7,4},{8,9},{9,10},{10,1... | collective-permute-start | bytes 442376 | tf_op jit(solution)/shard_map/ppermute | solution.py:478
  236.8 15.8 %collective-permute-start.45 = (bf16[24,3072]{1,0:T(8,128)(2,1)}, bf16[24,3072]{1,0:T(8,128)(2,1)}, u32[]{:S(2)}, u32[]{:S(2)}) collective-permute-start(bf16[24,3072]{1,0:T(8,128)(2,1)} %get-tuple-element.304), channel_id=1, source_target_pairs={{0,2},{1,3},{2,0},{3,1},{4,6},{5,7},{6,4},{7,5},{8,10},{9,11},{10,... | collective-permute-start | bytes 442376 | tf_op jit(solution)/shard_map/ppermute | solution.py:478
  238.5 14.1 %collective-permute-start.46 = (bf16[24,3072]{1,0:T(8,128)(2,1)}, bf16[24,3072]{1,0:T(8,128)(2,1)}, u32[]{:S(2)}, u32[]{:S(2)}) collective-permute-start(bf16[24,3072]{1,0:T(8,128)(2,1)} %get-tuple-element.303), channel_id=1, source_target_pairs={{0,3},{1,0},{2,1},{3,2},{4,7},{5,4},{6,5},{7,6},{8,11},{9,8},{10,9... | collective-permute-start | bytes 442376 | tf_op jit(solution)/shard_map/ppermute | solution.py:478
  240.3 25.6 %collective-permute-start.49 = (bf16[96,1920]{1,0:T(8,128)(2,1)}, bf16[96,1920]{1,0:T(8,128)(2,1)}, u32[]{:S(2)}, u32[]{:S(2)}) collective-permute-start(bf16[96,1920]{1,0:T(8,128)(2,1)} %get-tuple-element.299), channel_id=1, source_target_pairs={{0,16},{1,17},{2,18},{3,19},{4,12},{5,13},{6,14},{7,15},{8,24},{9,... | collective-permute-start | bytes 1105928 | tf_op jit(solution)/shard_map/ppermute | solution.py:474
  251.0 15.0 %collective-permute-start.48 = (bf16[96,1920]{1,0:T(8,128)(2,1)}, bf16[96,1920]{1,0:T(8,128)(2,1)S(1)}, u32[]{:S(2)}, u32[]{:S(2)}) collective-permute-start(bf16[96,1920]{1,0:T(8,128)(2,1)} %fusion.19), channel_id=1, source_target_pairs={{0,8},{1,9},{2,10},{3,11},{4,20},{5,21},{6,22},{7,23},{8,0},{9,1},... | collective-permute-start | bytes 1105928 | tf_op jit(solution)/shard_map/ppermute | solution.py:474
  257.4 36.8 %all-to-all-start = ((f32[32,24,128]{2,1,0:T(8,128)}), f32[32,24,128]{2,1,0:T(8,128)S(1)}, u32[]{:S(2)}, u32[]{:S(2)}) async-start(f32[32,24,128]{2,1,0:T(8,128)} %payload.1), calls=%async_computation | async-start | bytes 786432 | tf_op jit(solution)/shard_map/all_to_all | solution.py:706
  261.9 7.8 %collective-permute-start.47 = (bf16[96,1152]{1,0:T(8,128)(2,1)S(1)}, bf16[96,1152]{1,0:T(8,128)(2,1)S(1)}, u32[]{:S(2)}, u32[]{:S(2)}) collective-permute-start(bf16[96,1152]{1,0:T(8,128)(2,1)S(1)} %get-tuple-element.302), channel_id=1, source_target_pairs={{0,16},{1,17},{2,18},{3,19},{4,12},{5,13},{6,14},{7,15},{8,24},{9,... | collective-permute-start | bytes 663560 | tf_op jit(solution)/shard_map/ppermute | solution.py:474
  263.8 19.5 %collective-permute-start.53 = (bf16[96,1152]{1,0:T(8,128)(2,1)S(1)}, bf16[96,1152]{1,0:T(8,128)(2,1)S(1)}, u32[]{:S(2)}, u32[]{:S(2)}) collective-permute-start(bf16[96,1152]{1,0:T(8,128)(2,1)S(1)} %get-tuple-element.301), channel_id=1, source_target_pairs={{0,16},{1,17},{2,18},{3,19},{4,12},{5,13},{6,14},{7,15},{8,24},{9,... | collective-permute-start | bytes 663560 | tf_op jit(solution)/shard_map/ppermute | solution.py:474
  271.2 7.5 %collective-permute-start.52 = (bf16[24,1920]{1,0:T(8,128)(2,1)S(1)}, bf16[24,1920]{1,0:T(8,128)(2,1)S(1)}, u32[]{:S(2)}, u32[]{:S(2)}) collective-permute-start(bf16[24,1920]{1,0:T(8,128)(2,1)S(1)} %get-tuple-element.310), channel_id=1, source_target_pairs={{0,3},{1,0},{2,1},{3,2},{4,7},{5,4},{6,5},{7,6},{8,11},{9,8},{10,9... | collective-permute-start | bytes 276488 | tf_op jit(solution)/shard_map/ppermute | solution.py:478
  275.0 8.2 %collective-permute-start.51 = (bf16[24,1920]{1,0:T(8,128)(2,1)S(1)}, bf16[24,1920]{1,0:T(8,128)(2,1)S(1)}, u32[]{:S(2)}, u32[]{:S(2)}) collective-permute-start(bf16[24,1920]{1,0:T(8,128)(2,1)S(1)} %get-tuple-element.311), channel_id=1, source_target_pairs={{0,2},{1,3},{2,0},{3,1},{4,6},{5,7},{6,4},{7,5},{8,10},{9,11},{10,... | collective-permute-start | bytes 276488 | tf_op jit(solution)/shard_map/ppermute | solution.py:478
  275.0 8.2 %collective-permute-start.50 = (bf16[24,1920]{1,0:T(8,128)(2,1)S(1)}, bf16[24,1920]{1,0:T(8,128)(2,1)S(1)}, u32[]{:S(2)}, u32[]{:S(2)}) collective-permute-start(bf16[24,1920]{1,0:T(8,128)(2,1)S(1)} %get-tuple-element.309), channel_id=1, source_target_pairs={{0,1},{1,2},{2,3},{3,0},{4,5},{5,6},{6,7},{7,4},{8,9},{9,10},{10,1... | collective-permute-start | bytes 276488 | tf_op jit(solution)/shard_map/ppermute | solution.py:478
  (82 other events, 534.1 us)
